TPU v7x, 512 devices: a whole 4x8x8 slice. The times are simulated.
512 devices in a mesh: outer: 64 (over y_lo, z, core), inner: 8 (over y_hi, x).
Axes of the slice: x: 4, y: 8 (y_hi: 2, y_lo: 4; y = y_hi * 4 + y_lo), z: 8, core: 2. Of those that a mesh axis runs over, the one named last changes fastest.
Arguments:
- queries: float32 [64, 1024, 256], P('outer', 'inner'), may hold values from -120 to 120
- key_rows: float32 [64, 1024, 128], P('outer', 'inner'), may hold values from -4 to 4
- value_rows: float32 [64, 1024, 128], P('outer', 'inner'), may hold values from -6 to 6
- cotangent: float32 [64, 1024, 256], P('outer', 'inner'), may hold values from -6 to 6
- block_order: int32 [32], replicated, may hold values from 0 to 31, each once
Outputs:
- attended: float32 [64, 1024, 256], P('outer', 'inner')
- query_grad: float32 [64, 1024, 256], P('outer', 'inner')
- key_grad: float32 [64, 1024, 128], P('outer', 'inner')
- value_grad: float32 [64, 1024, 128], P('outer', 'inner')
Inputs may be any that keep to these rules, and one draw needn't show every extreme that they name: block_order is a permutation; stored block b of every sequence holds positions block_order[b] * 128 to block_order[b] * 128 + 127.
All inputs are finite; a program needn't handle non-finite values.
Results may differ from a plain program's by a relative error of at most 0.00055.
Values sent between devices are 32-bit elements; how exact they have to be, the bound alone decides.
A program may use at most 64 MiB of HBM per device.

v0:
```python
import jax
import jax.numpy as jnp
from jax import lax
from jax.sharding import PartitionSpec as P

HD = 128
HEADS = 2
GROUPS = 4


HIGH = lax.Precision.HIGHEST


def shifted(value, axis, steps):
    count = lax.axis_size(axis)
    pairs = [(source, (source + steps) % count) for source in range(count)]
    return lax.ppermute(value, axis, pairs)


def split_heads(tile_data):
    tokens = tile_data.shape[0]
    return tile_data.reshape(tokens, HEADS, HD).transpose(1, 0, 2).reshape(HEADS * tokens, HD)


def merge_heads(stacked):
    tokens = stacked.shape[0] // HEADS
    return stacked.reshape(HEADS, tokens, HD).transpose(1, 0, 2).reshape(tokens, HEADS * HD)


def lookup_order(block_order, indices):
    table_ids = jnp.arange(block_order.shape[0], dtype=jnp.int32)
    return jnp.sum(
        jnp.where(indices[:, None] == table_ids[None, :], block_order[None, :], 0), axis=1
    )


def key_positions(block_order, source, count, tok, n_inner):
    offsets = jnp.arange(count, dtype=jnp.int32)
    blocks_at = source * n_inner + offsets // tok
    return lookup_order(block_order, blocks_at) * tok + offsets % tok


def forward_tile(carry, query_rows, query_pos, slab, slab_pos):
    running_max, running_sum, running_out = carry
    scores = jnp.dot(
        query_rows, slab[0].T, precision=HIGH, preferred_element_type=jnp.float32
    ) * HD ** (-0.5)
    visible = slab_pos[None, :] <= query_pos[:, None]
    scores = jnp.where(visible, scores, -jnp.inf)
    new_max = jnp.maximum(running_max, jnp.max(scores, axis=1))
    safe_max = jnp.where(new_max == -jnp.inf, 0.0, new_max)
    weights = jnp.exp(scores - safe_max[:, None])
    factor = jnp.exp(running_max - safe_max)
    running_sum = factor * running_sum + jnp.sum(weights, axis=1)
    running_out = factor[:, None] * running_out + jnp.dot(
        weights, slab[1], precision=HIGH, preferred_element_type=jnp.float32
    )
    return (new_max, running_sum, running_out)


def backward_tile(query_rows, grad_rows, log_total, row_dot, query_pos, slab, slab_pos):
    scale = HD ** (-0.5)
    scores = (
        jnp.dot(query_rows, slab[0].T, precision=HIGH, preferred_element_type=jnp.float32) * scale
    )
    visible = slab_pos[None, :] <= query_pos[:, None]
    weights = jnp.exp(jnp.where(visible, scores, -jnp.inf) - log_total[:, None])
    grad_weights = jnp.dot(grad_rows, slab[1].T, precision=HIGH, preferred_element_type=jnp.float32)
    grad_scores = weights * (grad_weights - row_dot[:, None])
    query_part = (
        jnp.dot(grad_scores, slab[0], precision=HIGH, preferred_element_type=jnp.float32) * scale
    )
    key_part = (
        jnp.dot(grad_scores.T, query_rows, precision=HIGH, preferred_element_type=jnp.float32)
        * scale
    )
    value_part = jnp.dot(weights.T, grad_rows, precision=HIGH, preferred_element_type=jnp.float32)
    return (query_part, jnp.stack([key_part, value_part]))


def visit_forward(carry, query_rows, query_pos, slab, slab_pos):
    return forward_tile(carry, query_rows, query_pos, slab, slab_pos)


def visit_backward(
    query_grad, query_rows, grad_rows, log_total, row_dot, query_pos, slab, slab_pos
):
    query_part, grads = backward_tile(
        query_rows, grad_rows, log_total, row_dot, query_pos, slab, slab_pos
    )
    return (query_grad + query_part, grads)


def body(queries, key_rows, value_rows, cotangent, block_order):
    tok = key_rows.shape[1]
    n_inner = lax.axis_size("inner")
    seqs = lax.axis_size("outer") // GROUPS
    group = lax.axis_index("outer") // seqs
    own_block = group * n_inner + lax.axis_index("inner")
    own_pos = lookup_order(block_order, jnp.reshape(own_block, (1,)))[0] * tok + jnp.arange(
        tok, dtype=jnp.int32
    )
    query_pos = jnp.tile(own_pos, HEADS)
    query_rows = split_heads(queries[0])
    grad_rows = split_heads(cotangent[0])
    own_pair = jnp.stack([key_rows[0], value_rows[0]])
    total_rows = query_rows.shape[0]
    carry = (
        jnp.full((total_rows,), -jnp.inf, jnp.float32),
        jnp.zeros((total_rows,), jnp.float32),
        jnp.zeros((total_rows, HD), jnp.float32),
    )
    kept = []
    own_slab = lax.all_gather(own_pair, "inner", axis=1, tiled=True)
    slab = own_slab
    for step in range(GROUPS):
        source = (group - step) % GROUPS
        kept.append(slab)
        slab_pos = key_positions(block_order, source, slab.shape[1], tok, n_inner)
        carry = visit_forward(carry, query_rows, query_pos, slab, slab_pos)
        if step + 1 < GROUPS:
            slab = shifted(slab, "outer", seqs)
    running_max, running_sum, running_out = carry
    attended_rows = running_out / running_sum[:, None]
    log_total = running_max + jnp.log(running_sum)
    row_dot = jnp.sum(grad_rows * attended_rows, axis=1)
    query_grad = jnp.zeros((total_rows, HD), jnp.float32)
    slab = own_slab
    accum = jnp.zeros(own_slab.shape, jnp.float32)
    for step in range(GROUPS):
        source = (group - step) % GROUPS
        if step > 0:
            slab, accum = shifted((slab, accum), "outer", seqs)
        slab_pos = key_positions(block_order, source, slab.shape[1], tok, n_inner)
        query_grad, grads = visit_backward(
            query_grad, query_rows, grad_rows, log_total, row_dot, query_pos, slab, slab_pos
        )
        accum = accum + grads
    accum = shifted(accum, "outer", seqs)
    own_grads = lax.psum_scatter(accum, "inner", scatter_dimension=1, tiled=True)
    return (
        merge_heads(attended_rows)[None],
        merge_heads(query_grad)[None],
        own_grads[0][None],
        own_grads[1][None],
    )


def solution(mesh):
    placed = (
        P("outer", "inner", None),
        P("outer", "inner", None),
        P("outer", "inner", None),
        P("outer", "inner", None),
        P(),
    )
    return jax.shard_map(
        body,
        mesh=mesh,
        in_specs=placed,
        out_specs=(
            P("outer", "inner", None),
            P("outer", "inner", None),
            P("outer", "inner", None),
            P("outer", "inner", None),
        ),
        check_vma=False,
    )
```

profile of v0, /device:TPU:1, one launch (start us, length us, event | category | flops | bytes accessed | tf_op | source)
XLA Modules:
  0.0 366.4 jit_solution(7974305500504001266)
XLA Ops:
  7.2 0.0 all-gather.2.cloned.1.call-start
  7.2 1.5 pad_maximum_fusion.1
  8.8 0.0 reduce-scatter.2.cloned.1.call-start
  8.8 72.3 %all-gather.2.cloned.1.call-done = f32[2,1024,128]{2,1,0:T(8,128)} async-done(((f32[2,128,128]{2,1,0:T(8,128)}), f32[2,1024,128]{2,1,0:T(8,128)}) %all-gather.2.cloned.1.call-update) | async-done | bytes 1048592 | tf_op jit(solution)/shard_map/all_gather | solution.py:114
  81.1 4.3 %collective-permute-start = (f32[2,1024,128]{2,1,0:T(8,128)}, f32[2,1024,128]{2,1,0:T(8,128)S(1)}, u32[]{:S(2)}, u32[]{:S(2)}) collective-permute-start(f32[2,1024,128]{2,1,0:T(8,128)} %all-gather.2.cloned.1.call-done), channel_id=1, source_target_pairs={{0,128},{8,136},{16,144},{24,152},{32,160},{40,168},{48,176},{56,1... | collective-permute-start | bytes 3145736 | tf_op jit(solution)/shard_map/ppermute | solution.py:17
  85.5 0.6 fusion.53
  86.8 20.6 %collective-permute-done = f32[2,1024,128]{2,1,0:T(8,128)S(1)} collective-permute-done((f32[2,1024,128]{2,1,0:T(8,128)}, f32[2,1024,128]{2,1,0:T(8,128)S(1)}, u32[]{:S(2)}, u32[]{:S(2)}) %collective-permute-start) | collective-permute-done | bytes 1048608 | tf_op jit(solution)/shard_map/ppermute | solution.py:17
  107.4 3.0 collective-permute-start.1
  110.5 0.2 select_reduce_fusion
  110.7 21.8 %collective-permute-done.1 = f32[2,1024,128]{2,1,0:T(8,128)S(1)} collective-permute-done((f32[2,1024,128]{2,1,0:T(8,128)S(1)}, f32[2,1024,128]{2,1,0:T(8,128)S(1)}, u32[]{:S(2)}, u32[]{:S(2)}) %collective-permute-start.1) | collective-permute-done | bytes 1048608 | tf_op jit(solution)/shard_map/ppermute | solution.py:17
  132.4 1.9 collective-permute-start.2
  134.3 0.6 broadcast_bitcast_fusion
  134.9 0.1 reshape_squeeze.7
  135.0 1.0 copy.20
  136.0 0.1 copy.21
  136.1 0.7 copy-done.7
  136.8 1.0 fusion.57
  137.8 1.0 fusion.58
  138.8 1.0 fusion.56
  139.8 16.8 %collective-permute-done.2 = f32[2,1024,128]{2,1,0:T(8,128)} collective-permute-done((f32[2,1024,128]{2,1,0:T(8,128)S(1)}, f32[2,1024,128]{2,1,0:T(8,128)}, u32[]{:S(2)}, u32[]{:S(2)}) %collective-permute-start.2) | collective-permute-done | bytes 1048608 | tf_op jit(solution)/shard_map/ppermute | solution.py:17
  156.6 2.0 fusion.55
  158.7 0.2 fusion.28
  158.9 0.2 fusion.27
  159.2 0.2 fusion.26
  159.4 0.2 fusion.25
  159.6 1.0 convolution_bitcast_fusion.3
  160.6 1.8 fusion.24
  162.5 1.8 fusion.23
  164.3 1.8 fusion.22
  166.1 3.1 multiply_reduce_fusion
  169.2 1.0 fusion.7
  170.3 1.0 fusion.16
  171.2 0.1 pad_maximum_fusion
  171.3 1.9 collective-permute-start.3
  173.3 1.0 fusion.5
  174.3 1.0 fusion.17
  175.3 1.0 convolution_bitcast_fusion.2
  176.3 18.3 %collective-permute-done.3 = f32[2,1024,128]{2,1,0:T(8,128)S(1)} collective-permute-done((f32[2,1024,128]{2,1,0:T(8,128)S(1)}, f32[2,1024,128]{2,1,0:T(8,128)S(1)}, u32[]{:S(2)}, u32[]{:S(2)}) %collective-permute-start.3) | collective-permute-done | bytes 1048608 | tf_op jit(solution)/shard_map/ppermute | solution.py:17
  194.5 0.1 maximum_add_fusion
  194.6 1.9 collective-permute-start.4
  196.6 1.0 fusion.3
  197.6 1.0 fusion.18
  198.6 1.0 convolution_bitcast_fusion.1
  199.6 17.3 %collective-permute-done.4 = f32[2,1024,128]{2,1,0:T(8,128)S(1)} collective-permute-done((f32[2,1024,128]{2,1,0:T(8,128)S(1)}, f32[2,1024,128]{2,1,0:T(8,128)S(1)}, u32[]{:S(2)}, u32[]{:S(2)}) %collective-permute-start.4) | collective-permute-done | bytes 1048608 | tf_op jit(solution)/shard_map/ppermute | solution.py:17
  216.9 0.1 maximum_add_fusion.1
  217.0 2.1 collective-permute-start.5
  219.2 2.0 fusion.1
  221.2 1.0 fusion.19
  222.2 1.0 convolution_bitcast_fusion
  223.2 15.3 %collective-permute-done.5 = f32[2,1024,128]{2,1,0:T(8,128)S(1)} collective-permute-done((f32[2,1024,128]{2,1,0:T(8,128)S(1)}, f32[2,1024,128]{2,1,0:T(8,128)S(1)}, u32[]{:S(2)}, u32[]{:S(2)}) %collective-permute-start.5) | collective-permute-done | bytes 1048608 | tf_op jit(solution)/shard_map/ppermute | solution.py:17
  238.5 0.1 maximum_add_fusion.2
  238.6 1.9 collective-permute-start.6
  240.6 19.7 %collective-permute-done.6 = f32[2,1024,128]{2,1,0:T(8,128)} collective-permute-done((f32[2,1024,128]{2,1,0:T(8,128)S(1)}, f32[2,1024,128]{2,1,0:T(8,128)}, u32[]{:S(2)}, u32[]{:S(2)}) %collective-permute-start.6) | collective-permute-done | bytes 1048608 | tf_op jit(solution)/shard_map/ppermute | solution.py:17
  260.3 0.0 reduce-scatter.2.cloned.1.call-update
  260.3 0.1 copy.22
  260.4 0.8 broadcast_in_dim_reshape.7
  261.2 3.2 fusion.37
  264.4 1.8 convolution_add_fusion.2
  266.2 1.8 convolution_add_fusion.1
  268.1 2.8 fusion.20
  270.9 0.1 copy.24
  271.0 0.8 broadcast_in_dim_reshape.8
  271.8 86.2 %reduce-scatter.2.cloned.1.call-done = f32[2,128,128]{2,1,0:T(8,128)} async-done(((f32[2,1024,128]{2,1,0:T(8,128)}), f32[2,128,128]{2,1,0:T(8,128)}) %reduce-scatter.2.cloned.1.call-update) | async-done | bytes 131088 | tf_op jit(solution)/shard_map/reduce_scatter | solution.py:140
  358.0 1.5 fusion.54
  (30 shorter events, 0.1 us)
Async XLA Ops:
  7.2 73.9 %all-gather.2.cloned.1.call-start = ((), (), s32[]{:S(2)}) async-start(), calls=%async_computation.1 | async-start | bytes 1179648 | tf_op jit(solution)/shard_map/all_gather | solution.py:114
  8.7 76.7 %copy-start.8 = (s32[32]{0:T(128)S(1)}, s32[32]{0:T(128)}, u32[]{:S(2)}) copy-start(s32[32]{0:T(128)} %param.9) | copy-start | bytes 388
  8.8 126.1 %copy-start.6 = (f32[1,128,256]{2,1,0:T(8,128)S(1)}, f32[1,128,256]{2,1,0:T(8,128)}, u32[]{:S(2)}) copy-start(f32[1,128,256]{2,1,0:T(8,128)} %param.8) | copy-start | bytes 393220
  8.8 349.2 %reduce-scatter.2.cloned.1.call-start = ((), (), s32[]{:S(2)}) async-start(), calls=%async_computation.2 | async-start | bytes 1179648 | tf_op jit(solution)/shard_map/reduce_scatter | solution.py:140
  81.1 55.0 %copy-start.1 = (f32[2,1024,128]{2,1,0:T(8,128)S(1)}, f32[2,1024,128]{2,1,0:T(8,128)}, u32[]{:S(2)}) copy-start(f32[2,1024,128]{2,1,0:T(8,128)} %all-gather.2.cloned.1.call-done) | copy-start | bytes 3145732
  81.1 26.3 %collective-permute-start = (f32[2,1024,128]{2,1,0:T(8,128)}, f32[2,1024,128]{2,1,0:T(8,128)S(1)}, u32[]{:S(2)}, u32[]{:S(2)}) collective-permute-start(f32[2,1024,128]{2,1,0:T(8,128)} %all-gather.2.cloned.1.call-done), channel_id=1, source_target_pairs={{0,128},{8,136},{16,144},{24,152},{32,160},{40,168},{48,176},{56,1... | collective-permute-start | bytes 3145736 | tf_op jit(solution)/shard_map/ppermute | solution.py:17
  107.4 65.9 %copy-start.2 = (f32[2,1024,128]{2,1,0:T(8,128)}, f32[2,1024,128]{2,1,0:T(8,128)S(1)}, u32[]{:S(2)}) copy-start(f32[2,1024,128]{2,1,0:T(8,128)S(1)} %collective-permute-done) | copy-start | bytes 3145732
  107.4 25.0 %collective-permute-start.1 = (f32[2,1024,128]{2,1,0:T(8,128)S(1)}, f32[2,1024,128]{2,1,0:T(8,128)S(1)}, u32[]{:S(2)}, u32[]{:S(2)}) collective-permute-start(f32[2,1024,128]{2,1,0:T(8,128)S(1)} %collective-permute-done), channel_id=1, source_target_pairs={{0,128},{8,136},{16,144},{24,152},{32,160},{40,168},{48,176},{56,1... | collective-permute-start | bytes 3145736 | tf_op jit(solution)/shard_map/ppermute | solution.py:17
  132.4 64.1 %copy-start.4 = (f32[2,1024,128]{2,1,0:T(8,128)}, f32[2,1024,128]{2,1,0:T(8,128)S(1)}, u32[]{:S(2)}) copy-start(f32[2,1024,128]{2,1,0:T(8,128)S(1)} %collective-permute-done.1) | copy-start | bytes 3145732
  132.4 24.2 %collective-permute-start.2 = (f32[2,1024,128]{2,1,0:T(8,128)S(1)}, f32[2,1024,128]{2,1,0:T(8,128)}, u32[]{:S(2)}, u32[]{:S(2)}) collective-permute-start(f32[2,1024,128]{2,1,0:T(8,128)S(1)} %collective-permute-done.1), channel_id=1, source_target_pairs={{0,128},{8,136},{16,144},{24,152},{32,160},{40,168},{48,176},{56,1... | collective-permute-start | bytes 3145736 | tf_op jit(solution)/shard_map/ppermute | solution.py:17
  136.1 0.7 copy-start.7
  170.2 1.1 copy-start
  171.3 23.2 %collective-permute-start.3 = (f32[2,1024,128]{2,1,0:T(8,128)S(1)}, f32[2,1024,128]{2,1,0:T(8,128)S(1)}, u32[]{:S(2)}, u32[]{:S(2)}) collective-permute-start(f32[2,1024,128]{2,1,0:T(8,128)S(1)} %pad_maximum_fusion), channel_id=1, source_target_pairs={{0,128},{8,136},{16,144},{24,152},{32,160},{40,168},{48,176},{56,1... | collective-permute-start | bytes 3145736 | tf_op jit(solution)/shard_map/ppermute | solution.py:17
  194.6 22.3 %collective-permute-start.4 = (f32[2,1024,128]{2,1,0:T(8,128)S(1)}, f32[2,1024,128]{2,1,0:T(8,128)S(1)}, u32[]{:S(2)}, u32[]{:S(2)}) collective-permute-start(f32[2,1024,128]{2,1,0:T(8,128)S(1)} %maximum_add_fusion), channel_id=1, source_target_pairs={{0,128},{8,136},{16,144},{24,152},{32,160},{40,168},{48,176},{56,1... | collective-permute-start | bytes 3145736 | tf_op jit(solution)/shard_map/ppermute | solution.py:17
  217.0 21.5 %collective-permute-start.5 = (f32[2,1024,128]{2,1,0:T(8,128)S(1)}, f32[2,1024,128]{2,1,0:T(8,128)S(1)}, u32[]{:S(2)}, u32[]{:S(2)}) collective-permute-start(f32[2,1024,128]{2,1,0:T(8,128)S(1)} %maximum_add_fusion.1), channel_id=1, source_target_pairs={{0,128},{8,136},{16,144},{24,152},{32,160},{40,168},{48,176},{56,1... | collective-permute-start | bytes 3145736 | tf_op jit(solution)/shard_map/ppermute | solution.py:17
  238.6 21.6 %collective-permute-start.6 = (f32[2,1024,128]{2,1,0:T(8,128)S(1)}, f32[2,1024,128]{2,1,0:T(8,128)}, u32[]{:S(2)}, u32[]{:S(2)}) collective-permute-start(f32[2,1024,128]{2,1,0:T(8,128)S(1)} %maximum_add_fusion.2), channel_id=1, source_target_pairs={{0,128},{8,136},{16,144},{24,152},{32,160},{40,168},{48,176},{56,1... | collective-permute-start | bytes 3145736 | tf_op jit(solution)/shard_map/ppermute | solution.py:17
  261.1 3.3 copy-start.3
  264.4 1.8 copy-start.5
Sparse Core Ops, SparseCore 0:
  11.8 69.2 all-gather.1
  260.4 97.5 reduce-scatter.1
where the time goes:
time: 367 us; the launch traced here: 366 us
  waiting for transfers between devices  288 us (78%)
  matrix products  36.3 us (10%)
  starting transfers between devices  17.2 us (5%)
  between operations  15.2 us (4%)
  local copies, waits for them, and re-layouts  5.69 us (2%)
  other arithmetic  3.67 us (1%)
    ppermute x7, waiting for transfers between devices, shifted(): return lax.ppermute(value, axis, pairs)  130 us
    reduce_scatter x1, waiting for transfers between devices, body(): lax.psum_scatter(accum, 'inner', scatter_dimension=1, tiled=True)  86.2 us
    all_gather x1, waiting for transfers between devices, body(): own_slab = lax.all_gather(own_pair, 'inner', axis=1, tiled=True)  72.3 us
    ppermute x7, starting transfers between devices, shifted(): return lax.ppermute(value, axis, pairs)  17.1 us
    dot_general x4, matrix products, backward_tile(): jnp.dot(grad_scores, slab[0], precision=HIGH, preferred_element_type=jnp....  9.7 us
    dot_general x4, matrix products, forward_tile(): jnp.dot(weights, slab[1], precision=HIGH, preferred_element_type=jnp.floa...  8.57 us
  transfers between devices with their start and end apart: 9, of which 9 were waited for; matrix products, arithmetic and copies ran while one was open for 7% of the time, Pallas kernels for 0%

commit v1 on v0

v1 whole, which is shorter than its diff:
```python
import jax
import jax.numpy as jnp
from jax import lax
from jax.experimental import pallas as pl
from jax.experimental.pallas import tpu as pltpu
from jax.sharding import PartitionSpec as P

HD = 128
HEADS = 2
GROUPS = 4
TOK = 128
NX = 4
NY = 8
QCOLS = HEADS * TOK
ALLQ = NX * QCOLS
ALLK = NY * TOK
HALF = TOK // 2
SCALE = HD ** (-0.5)
LOG2E = 1.4426950408889634
LN2 = 0.6931471805599453
FAR = -1e30
MESH = pl.DeviceIdType.MESH
F32 = jnp.float32
BF16 = jnp.bfloat16

AT = (0, 1, 7, 2, 6, 3, 5, 4)
PLACE = tuple(AT.index(r) for r in range(NY))
CHUNK = 2 * TOK


def split2(value):
    high = value.astype(BF16)
    return high, (value - high.astype(F32)).astype(BF16)


def split3(value):
    high = value.astype(BF16)
    rest = value - high.astype(F32)
    mid = rest.astype(BF16)
    return high, mid, (rest - mid.astype(F32)).astype(BF16)


def matmul(left, right):
    return jnp.dot(left, right, preferred_element_type=F32)


def matmul_nt(left, right):
    return lax.dot_general(left, right, (((1,), (1,)), ((), ())), preferred_element_type=F32)


def fold_rows(value, combine):
    return combine(value.reshape(value.shape[0] // 8, 8, value.shape[1]), axis=0)


def kernel(
    order, q_hbm, k_hbm, v_hbm, g_hbm, o_out, dq_out, dk_out, dv_out,
    q_own, g_own, q_t, g_t, keys, vals, qs, gs, kp, vp, kt, vt, qf, gf,
    scores, gw, p_hi, p_lo, t_hi, t_lo, max8, sum8, dot8, stats, dots, scaled,
    dv_part, dk_part, o_part, dq_part, dv_in, dv_half, dk_in, dk_half, o_in, o_half, dq_in, dq_half,
    local_sem, qx_s, qx_r, gx_s, gx_r, ky_s, ky_r, vy_s, vy_r, st_s, st_r, rd_s, rd_r,
    dvy_s, dvy_r, dky_s, dky_r, ox_s, ox_r, dqx_s, dqx_r,
):
    seqs = lax.axis_size("outer") // GROUPS
    outer = lax.axis_index("outer")
    inner = lax.axis_index("inner")
    seq = lax.rem(outer, seqs)
    x = lax.rem(inner, NX)
    y = (inner // NX) * GROUPS + outer // seqs

    def device(at_x, at_y):
        return (lax.rem(at_y, GROUPS) * seqs + seq, (at_y // GROUPS) * NX + at_x)

    def along_x(step):
        return device(lax.rem(x + step + NX, NX), y)

    def along_y(step):
        return device(x, lax.rem(y + step + NY, NY))

    def position(at_x, at_y):
        return order[lax.rem(at_y, GROUPS) * (NX * NY // GROUPS) + (at_y // GROUPS) * NX + at_x]

    def remote(src, dst, send, recv, where):
        return pltpu.make_async_remote_copy(
            src_ref=src, dst_ref=dst, send_sem=send, recv_sem=recv, device_id=where, device_id_type=MESH
        )

    up, down, right, left, across = along_y(1), along_y(-1), along_x(1), along_x(-1), along_x(2)
    peers = (right, across, left)

    loads = [
        pltpu.make_async_copy(q_hbm.at[0], q_own, local_sem.at[0]),
        pltpu.make_async_copy(g_hbm.at[0], g_own, local_sem.at[1]),
        pltpu.make_async_copy(k_hbm.at[0], keys.at[0], local_sem.at[2]),
        pltpu.make_async_copy(v_hbm.at[0], vals.at[0], local_sem.at[3]),
    ]
    for load in loads:
        load.start()
    barrier = pltpu.get_barrier_semaphore()
    for peer in (up, down, right, left, across):
        pl.semaphore_signal(barrier, inc=1, device_id=peer, device_id_type=MESH)
    loads[0].wait()
    for h in range(HEADS):
        q_t[0, :, h * TOK:(h + 1) * TOK] = q_own[:, h * HD:(h + 1) * HD].T * (SCALE * LOG2E)
    loads[1].wait()
    for h in range(HEADS):
        g_t[0, :, h * TOK:(h + 1) * TOK] = g_own[:, h * HD:(h + 1) * HD].T
    loads[2].wait()
    loads[3].wait()
    pl.semaphore_wait(barrier, 5)

    def ring_y(buf, send, recv):
        copies = {}
        for j in range(4):
            for d, (sign, where) in enumerate(((1, up), (-1, down))):
                src, dst = PLACE[(sign * j) % NY], PLACE[(sign * (j + 1)) % NY]
                rows = pl.ds(0, TOK) if j < 3 else pl.ds(d * HALF, HALF)
                n = 2 * j + d
                copies[j, d] = remote(buf.at[src, rows], buf.at[dst, rows], send.at[n], recv.at[n], where)
        return copies

    def ring_x(buf, send, recv):
        copies = {}
        for d, where in enumerate((right, left)):
            near = 1 if d == 0 else 3
            copies[0, d] = remote(buf.at[0], buf.at[near], send.at[d], recv.at[d], where)
            rows = pl.ds(d * HALF, HALF)
            copies[1, d] = remote(buf.at[near, rows], buf.at[2, rows], send.at[2 + d], recv.at[2 + d], where)
        return copies

    k_go, v_go = ring_y(keys, ky_s, ky_r), ring_y(vals, vy_s, vy_r)
    q_go, g_go = ring_x(q_t, qx_s, qx_r), ring_x(g_t, gx_s, gx_r)
    everything = [*k_go.values(), *v_go.values(), *q_go.values(), *g_go.values()]

    def pass_on(copies, j, last):
        for d in range(2):
            copies[j - 1, d].wait_recv()
            if j <= last:
                copies[j, d].start()

    def ready_query(s):
        cols = pl.ds(s * QCOLS, QCOLS)
        q0, q1, q2 = split3(q_t[s])
        for n, piece in enumerate((q0, q1, q0, q1, q0, q2)):
            qs[n * HD:(n + 1) * HD, cols] = piece

    def ready_cotangent(s):
        cols = pl.ds(s * QCOLS, QCOLS)
        g0, g1 = split2(g_t[s])
        for n, piece in enumerate((g0, g1, g0)):
            gs[n * HD:(n + 1) * HD, cols] = piece

    def ready_key(place):
        rows = pl.ds(place * TOK, TOK)
        k0, k1, k2 = split3(keys[place])
        for n, piece in enumerate((k0, k0, k1, k1, k2, k0)):
            kp[rows, n * HD:(n + 1) * HD] = piece
        high, low = split2(keys[place].T)
        kt[0:HD, rows] = high
        kt[HD:2 * HD, rows] = low

    def ready_value(place):
        rows = pl.ds(place * TOK, TOK)
        v0, v1 = split2(vals[place])
        for n, piece in enumerate((v0, v0, v1)):
            vp[rows, n * HD:(n + 1) * HD] = piece
        high, low = split2(vals[place].T)
        vt[0:HD, rows] = high
        vt[HD:2 * HD, rows] = low

    def score_chunk(c):
        rows = pl.ds(c * CHUNK, CHUNK)
        for s in range(NX):
            cols = pl.ds(s * QCOLS, QCOLS)
            query_at = position(lax.rem(x - s + NX, NX), y)
            tile = matmul(kp[rows, :], qs[:, cols])
            parts = []
            for n in range(2):
                r = AT[2 * c + n]
                part = tile[n * TOK:(n + 1) * TOK]
                if r == 0 and s == 0:
                    key_at = lax.broadcasted_iota(jnp.int32, (TOK, QCOLS), 0)
                    token = lax.rem(lax.broadcasted_iota(jnp.int32, (TOK, QCOLS), 1), TOK)
                    part = jnp.where(key_at <= token, part, FAR)
                else:
                    seen = position(x, lax.rem(y - r + NY, NY)) <= query_at
                    part = part + jnp.where(seen, 0.0, FAR).astype(F32)
                parts.append(part)
            for n, part in enumerate(parts):
                scores[c * CHUNK + n * TOK:c * CHUNK + (n + 1) * TOK, cols] = part
            top = jnp.maximum(fold_rows(parts[0], jnp.max), fold_rows(parts[1], jnp.max))
            max8[:, cols] = top if c == 0 else jnp.maximum(max8[:, cols], top)

    for d in range(2):
        k_go[0, d].start()
        q_go[0, d].start()
    for d in range(2):
        v_go[0, d].start()
        g_go[0, d].start()
    ready_query(0)
    ready_key(0)
    ready_cotangent(0)
    ready_value(0)

    pass_on(k_go, 1, 3)
    ready_key(1)
    ready_key(2)
    pass_on(q_go, 1, 1)
    ready_query(1)
    ready_query(3)
    pass_on(v_go, 1, 3)
    pass_on(k_go, 2, 3)
    ready_key(3)
    ready_key(4)
    pass_on(g_go, 1, 1)
    pass_on(q_go, 2, 1)
    ready_query(2)
    score_chunk(0)
    pass_on(v_go, 2, 3)
    score_chunk(1)
    pass_on(k_go, 3, 3)
    ready_key(5)
    ready_key(6)
    score_chunk(2)
    pass_on(v_go, 3, 3)
    pass_on(k_go, 4, 3)
    ready_key(7)
    score_chunk(3)

    top = jnp.max(max8[...], axis=0, keepdims=True)
    for c in range(NY // 2):
        rows = pl.ds(c * CHUNK, CHUNK)
        for s in range(NX):
            cols = pl.ds(s * QCOLS, QCOLS)
            weight = jnp.exp2(scores[rows, cols] - top[:, s * QCOLS:(s + 1) * QCOLS])
            scores[rows, cols] = weight
            high, low = split2(weight)
            p_hi[rows, cols] = high
            p_lo[rows, cols] = low
            part = fold_rows(weight, jnp.sum)
            sum8[:, cols] = part if c == 0 else sum8[:, cols] + part
    stats[0, 0:1, :] = top
    stats[0, 1:2, :] = jnp.sum(sum8[...], axis=0, keepdims=True)
    st_go = [
        remote(stats.at[0], stats.at[n + 1], st_s.at[n], st_r.at[n], peers[n]) for n in range(NX - 1)
    ]
    for copy in st_go:
        copy.start()

    pass_on(g_go, 2, 1)
    for s in (1, 3, 2):
        ready_cotangent(s)
    for place in range(1, 5):
        ready_value(place)

    def weigh_chunk(c):
        rows = pl.ds(c * CHUNK, CHUNK)
        for s in range(NX):
            cols = pl.ds(s * QCOLS, QCOLS)
            tile = matmul(vp[rows, :], gs[:, cols])
            gw[rows, cols] = tile
            part = fold_rows(tile * scores[rows, cols], jnp.sum)
            dot8[:, cols] = part if c == 0 else dot8[:, cols] + part

    weigh_chunk(0)
    weigh_chunk(1)

    def aligned(row, n):
        cut = ALLQ - (n + 1) * QCOLS
        return jnp.concatenate([row[:, cut:], row[:, :cut]], axis=1)

    for copy in st_go:
        copy.wait_recv()
    tops = [aligned(stats[n + 1, 0:1, :], n) for n in range(NX - 1)]
    whole_top = jnp.maximum(jnp.maximum(top, tops[0]), jnp.maximum(tops[1], tops[2]))
    own_factor = jnp.exp2(top - whole_top)
    total = own_factor * stats[0, 1:2, :]
    for n in range(NX - 1):
        total = total + jnp.exp2(tops[n] - whole_top) * aligned(stats[n + 1, 1:2, :], n)
    factor = own_factor / total
    scaled[...] = factor

    for s in range(NX):
        cols = pl.ds(s * QCOLS, QCOLS)
        row = scaled[:, cols]
        high, low = split2(g_t[s] * row)
        gf[0:HD, cols] = high
        gf[HD:2 * HD, cols] = low
        high, low = split2(q_t[s] * row)
        qf[0:HD, cols] = high
        qf[HD:2 * HD, cols] = low

    def key_side(c, high, low, right_side, part):
        rows = pl.ds(c * CHUNK, CHUNK)
        both = matmul_nt(high[rows, :], right_side[...]) + matmul_nt(low[rows, :], right_side[...])
        whole = both[:, :HD] + both[:, HD:]
        part[2 * c] = whole[:TOK]
        part[2 * c + 1] = whole[TOK:]

    def back_y(part, full_in, half_in, send, recv):
        copies = {}
        for d, (sign, where) in enumerate(((-1, down), (1, up))):
            rows = pl.ds(d * HALF, HALF)
            for j, n in enumerate((4, 3, 2, 1)):
                src = part.at[PLACE[(-sign * n) % NY]]
                if j == 0:
                    copies[j, d] = remote(src.at[rows], half_in.at[d], send.at[d], recv.at[d], where)
                else:
                    at = 2 * j + d
                    copies[j, d] = remote(src, full_in.at[2 * (j - 1) + d], send.at[at], recv.at[at], where)
        return copies

    def join_y(copies, j, part, full_in, half_in):
        for d, sign in enumerate((-1, 1)):
            place = PLACE[(-sign * (4 - j)) % NY]
            copies[j - 1, d].wait_recv()
            if j == 1:
                rows = pl.ds(d * HALF, HALF)
                part[place, rows, :] = part[place, rows, :] + half_in[d]
            else:
                part[place] = part[place] + full_in[2 * (j - 2) + d]
            if j < 4:
                copies[j, d].start()

    def back_x(part, full_in, half_in, send, recv):
        copies = {}
        for d, where in enumerate((right, left)):
            rows = pl.ds(d * HALF, HALF)
            near = 3 if d == 0 else 1
            copies[0, d] = remote(part.at[2, rows], half_in.at[d], send.at[d], recv.at[d], where)
            copies[1, d] = remote(part.at[near], full_in.at[d], send.at[2 + d], recv.at[2 + d], where)
        return copies

    def join_x(copies, part, half_in):
        for d in range(2):
            near = 3 if d == 0 else 1
            rows = pl.ds(d * HALF, HALF)
            copies[0, d].wait_recv()
            part[near, rows, :] = part[near, rows, :] + half_in[d]
            copies[1, d].start()

    dv_go = back_y(dv_part, dv_in, dv_half, dvy_s, dvy_r)
    dk_go = back_y(dk_part, dk_in, dk_half, dky_s, dky_r)
    o_go = back_x(o_part, o_in, o_half, ox_s, ox_r)
    dq_go = back_x(dq_part, dq_in, dq_half, dqx_s, dqx_r)
    everything += [*st_go, *dv_go.values(), *dk_go.values(), *o_go.values(), *dq_go.values()]

    key_side(3, p_hi, p_lo, gf, dv_part)
    for d in range(2):
        dv_go[0, d].start()

    ready_value(5)
    ready_value(6)
    weigh_chunk(2)
    pass_on(v_go, 4, 3)
    ready_value(7)
    weigh_chunk(3)
    dots[0] = jnp.sum(dot8[...], axis=0, keepdims=True) * scaled[...]
    rd_go = [
        remote(dots.at[0], dots.at[n + 1], rd_s.at[n], rd_r.at[n], peers[n]) for n in range(NX - 1)
    ]
    everything += rd_go
    for copy in rd_go:
        copy.start()

    key_side(2, p_hi, p_lo, gf, dv_part)
    join_y(dv_go, 1, dv_part, dv_in, dv_half)

    def query_side(s, sides, high, low, part, scale):
        cols = pl.ds(s * QCOLS, QCOLS)
        both = matmul(sides[...], high[:, cols]) + matmul(sides[...], low[:, cols])
        part[s] = (both[:HD] + both[HD:]) * (scaled[:, cols] * scale)

    query_side(2, vt, p_hi, p_lo, o_part, 1.0)
    for d in range(2):
        o_go[0, d].start()
    key_side(1, p_hi, p_lo, gf, dv_part)
    join_y(dv_go, 2, dv_part, dv_in, dv_half)
    query_side(1, vt, p_hi, p_lo, o_part, 1.0)
    query_side(3, vt, p_hi, p_lo, o_part, 1.0)
    join_x(o_go, o_part, o_half)
    key_side(0, p_hi, p_lo, gf, dv_part)
    join_y(dv_go, 3, dv_part, dv_in, dv_half)

    for copy in rd_go:
        copy.wait_recv()
    row_dot = dots[0]
    for n in range(NX - 1):
        row_dot = row_dot + aligned(dots[n + 1], n)

    def grad_chunk(c):
        rows = pl.ds(c * CHUNK, CHUNK)
        for s in range(NX):
            cols = pl.ds(s * QCOLS, QCOLS)
            value = scores[rows, cols] * (gw[rows, cols] - row_dot[:, s * QCOLS:(s + 1) * QCOLS])
            high, low = split2(value)
            t_hi[rows, cols] = high
            t_lo[rows, cols] = low

    grad_chunk(3)
    key_side(3, t_hi, t_lo, qf, dk_part)
    for d in range(2):
        dk_go[0, d].start()
    grad_chunk(2)
    key_side(2, t_hi, t_lo, qf, dk_part)
    join_y(dk_go, 1, dk_part, dk_in, dk_half)
    grad_chunk(1)
    grad_chunk(0)
    query_side(2, kt, t_hi, t_lo, dq_part, SCALE)
    for d in range(2):
        dq_go[0, d].start()
    key_side(1, t_hi, t_lo, qf, dk_part)
    join_y(dk_go, 2, dk_part, dk_in, dk_half)
    query_side(1, kt, t_hi, t_lo, dq_part, SCALE)
    query_side(3, kt, t_hi, t_lo, dq_part, SCALE)
    join_x(dq_go, dq_part, dq_half)
    key_side(0, t_hi, t_lo, qf, dk_part)
    join_y(dk_go, 3, dk_part, dk_in, dk_half)
    query_side(0, vt, p_hi, p_lo, o_part, 1.0)
    query_side(0, kt, t_hi, t_lo, dq_part, SCALE)

    def finish_x(copies, part, full_in, out):
        for d in range(2):
            copies[1, d].wait_recv()
        whole = part[0] + full_in[0] + full_in[1]
        for h in range(HEADS):
            out[0, :, h * HD:(h + 1) * HD] = whole[:, h * TOK:(h + 1) * TOK].T

    finish_x(o_go, o_part, o_in, o_out)
    join_y(dv_go, 4, dv_part, dv_in, dv_half)
    dv_out[0] = dv_part[0]
    finish_x(dq_go, dq_part, dq_in, dq_out)
    join_y(dk_go, 4, dk_part, dk_in, dk_half)
    dk_out[0] = dk_part[0] * LN2
    for copy in everything:
        copy.wait_send()


def body(queries, key_rows, value_rows, cotangent, block_order):
    def vmem(*shape, dtype=F32):
        return pltpu.VMEM(shape, dtype)

    dma = lambda n: pltpu.SemaphoreType.DMA((n,))
    in_vmem = pl.BlockSpec(memory_space=pltpu.VMEM)
    anywhere = pl.BlockSpec(memory_space=pl.ANY)
    wide = jax.ShapeDtypeStruct((1, TOK, HEADS * HD), F32)
    narrow = jax.ShapeDtypeStruct((1, TOK, HD), F32)
    return pl.pallas_call(
        kernel,
        out_shape=(wide, wide, narrow, narrow),
        in_specs=[pl.BlockSpec(memory_space=pltpu.SMEM)] + [anywhere] * 4,
        out_specs=[in_vmem] * 4,
        scratch_shapes=[
            vmem(TOK, HEADS * HD), vmem(TOK, HEADS * HD),
            vmem(NX, HD, QCOLS), vmem(NX, HD, QCOLS),
            vmem(NY, TOK, HD), vmem(NY, TOK, HD),
            vmem(6 * HD, ALLQ, dtype=BF16), vmem(3 * HD, ALLQ, dtype=BF16),
            vmem(ALLK, 6 * HD, dtype=BF16), vmem(ALLK, 3 * HD, dtype=BF16),
            vmem(2 * HD, ALLK, dtype=BF16), vmem(2 * HD, ALLK, dtype=BF16),
            vmem(2 * HD, ALLQ, dtype=BF16), vmem(2 * HD, ALLQ, dtype=BF16),
            vmem(ALLK, ALLQ), vmem(ALLK, ALLQ),
            vmem(ALLK, ALLQ, dtype=BF16), vmem(ALLK, ALLQ, dtype=BF16),
            vmem(ALLK, ALLQ, dtype=BF16), vmem(ALLK, ALLQ, dtype=BF16),
            vmem(8, ALLQ), vmem(8, ALLQ), vmem(8, ALLQ),
            vmem(NX, 2, ALLQ), vmem(NX, 1, ALLQ), vmem(1, ALLQ),
            vmem(NY, TOK, HD), vmem(NY, TOK, HD),
            vmem(NX, HD, QCOLS), vmem(NX, HD, QCOLS),
            vmem(6, TOK, HD), vmem(2, HALF, HD), vmem(6, TOK, HD), vmem(2, HALF, HD),
            vmem(2, HD, QCOLS), vmem(2, HALF, QCOLS), vmem(2, HD, QCOLS), vmem(2, HALF, QCOLS),
            dma(4),
            dma(4), dma(4), dma(4), dma(4), dma(8), dma(8), dma(8), dma(8),
            dma(3), dma(3), dma(3), dma(3),
            dma(8), dma(8), dma(8), dma(8), dma(4), dma(4), dma(4), dma(4),
        ],
        compiler_params=pltpu.CompilerParams(
            collective_id=0, has_side_effects=True, vmem_limit_bytes=52 * 1024 * 1024
        ),
    )(block_order, queries, key_rows, value_rows, cotangent)


def solution(mesh):
    spread = P("outer", "inner", None)
    return jax.shard_map(
        body,
        mesh=mesh,
        in_specs=(spread, spread, spread, spread, P()),
        out_specs=(spread, spread, spread, spread),
        check_vma=False,
    )
```

time: 367 us -> 64.2 us (0.17)
  the two profiles are of different devices: /device:TPU:1 before, /device:TPU:384 now
where the time goes in v1:
time: 64.2 us; the launch traced here: 64 us
  Pallas kernels  56.6 us (88%)
  local copies, waits for them, and re-layouts  6.7 us (10%)
  between operations  0.65 us (1%)
    pallas_call x1, Pallas kernels, body(): pl.pallas_call(kernel, out_shape=(wide, wide, narrow, narrow), in_specs=[...  56.6 us
    unnamed x14, local copies, waits for them, and re-layouts  6.7 us

profile of v1, /device:TPU:384, one launch (start us, length us, event | category | flops | bytes accessed | tf_op | source)
XLA Modules:
  0.0 64.0 jit_solution(9747019023461942826)
XLA Ops:
  0.6 0.0 copy-start
  0.6 0.9 %copy-done = f32[1,128,256]{2,1,0:T(8,128)S(1)} copy-done((f32[1,128,256]{2,1,0:T(8,128)S(1)}, f32[1,128,256]{2,1,0:T(8,128)}, u32[]{:S(2)}) %copy-start) | copy-done | bytes 131096
  1.5 0.0 copy-start.1
  1.5 0.9 %copy-done.1 = f32[1,128,256]{2,1,0:T(8,128)S(1)} copy-done((f32[1,128,256]{2,1,0:T(8,128)S(1)}, f32[1,128,256]{2,1,0:T(8,128)}, u32[]{:S(2)}) %copy-start.1) | copy-done | bytes 131096
  2.4 0.0 copy-start.2
  2.4 0.8 %copy-done.2 = f32[1,128,128]{2,1,0:T(8,128)S(1)} copy-done((f32[1,128,128]{2,1,0:T(8,128)S(1)}, f32[1,128,128]{2,1,0:T(8,128)}, u32[]{:S(2)}) %copy-start.2) | copy-done | bytes 65560
  3.3 0.0 copy-start.3
  3.3 0.8 %copy-done.3 = f32[1,128,128]{2,1,0:T(8,128)S(1)} copy-done((f32[1,128,128]{2,1,0:T(8,128)S(1)}, f32[1,128,128]{2,1,0:T(8,128)}, u32[]{:S(2)}) %copy-start.3) | copy-done | bytes 65560
  4.1 0.0 copy-start.4
  4.1 0.7 %copy-done.4 = s32[32]{0:T(128)S(1)} copy-done((s32[32]{0:T(128)S(1)}, s32[32]{0:T(128)}, u32[]{:S(2)}) %copy-start.4) | copy-done | bytes 152
  4.8 56.6 %shard_map.84 = (f32[1,128,256]{2,1,0:T(8,128)S(1)}, f32[1,128,256]{2,1,0:T(8,128)S(1)}, f32[1,128,128]{2,1,0:T(8,128)S(1)}, f32[1,128,128]{2,1,0:T(8,128)S(1)}) custom-call(s32[32]{0:T(128)S(1)} %copy-done.4, f32[1,128,256]{2,1,0:T(8,128)S(1)} %copy-done, f32[1,128,128]{2,1,0:T(8,128)S(1)} %copy-done.2, f32[1,128,128]{2,1,0:T(8,128)S(1)} %copy-done.3, ...), custom_call_target="tpu_custom_call" | custom-call | tf_op jit(solution)/shard_map/pallas_call | solution.py:447
  61.4 0.7 %copy.13 = f32[1,128,256]{2,1,0:T(8,128)} copy(f32[1,128,256]{2,1,0:T(8,128)S(1)} %get-tuple-element.8) | data formatting | bytes 262144
  62.1 0.7 %copy.14 = f32[1,128,256]{2,1,0:T(8,128)} copy(f32[1,128,256]{2,1,0:T(8,128)S(1)} %get-tuple-element.9) | data formatting | bytes 262144
  62.7 0.6 copy.15
  63.4 0.6 copy.16
Async XLA Ops:
  0.6 0.9 %copy-start = (f32[1,128,256]{2,1,0:T(8,128)S(1)}, f32[1,128,256]{2,1,0:T(8,128)}, u32[]{:S(2)}) copy-start(f32[1,128,256]{2,1,0:T(8,128)} %q_hbm.1) | copy-start | bytes 393220
  1.5 0.9 %copy-start.1 = (f32[1,128,256]{2,1,0:T(8,128)S(1)}, f32[1,128,256]{2,1,0:T(8,128)}, u32[]{:S(2)}) copy-start(f32[1,128,256]{2,1,0:T(8,128)} %g_hbm.1) | copy-start | bytes 393220
  2.4 0.8 %copy-start.2 = (f32[1,128,128]{2,1,0:T(8,128)S(1)}, f32[1,128,128]{2,1,0:T(8,128)}, u32[]{:S(2)}) copy-start(f32[1,128,128]{2,1,0:T(8,128)} %k_hbm.1) | copy-start | bytes 196612
  3.3 0.8 %copy-start.3 = (f32[1,128,128]{2,1,0:T(8,128)S(1)}, f32[1,128,128]{2,1,0:T(8,128)}, u32[]{:S(2)}) copy-start(f32[1,128,128]{2,1,0:T(8,128)} %v_hbm.1) | copy-start | bytes 196612
  4.1 0.7 %copy-start.4 = (s32[32]{0:T(128)S(1)}, s32[32]{0:T(128)}, u32[]{:S(2)}) copy-start(s32[32]{0:T(128)} %order.1) | copy-start | bytes 388

commit v2 on v1

v2 whole, which is shorter than its diff:
```python
import jax
import jax.numpy as jnp
from jax import lax
from jax.experimental import pallas as pl
from jax.experimental.pallas import tpu as pltpu
from jax.sharding import PartitionSpec as P

HD = 128
HEADS = 2
GROUPS = 4
TOK = 128
NX = 4
NY = 8
QCOLS = HEADS * TOK
ALLQ = NX * QCOLS
ALLK = NY * TOK
HALF = TOK // 2
SCALE = HD ** (-0.5)
LOG2E = 1.4426950408889634
LN2 = 0.6931471805599453
FAR = -1e30
MESH = pl.DeviceIdType.MESH
F32 = jnp.float32
BF16 = jnp.bfloat16

AT = (2, 6, 1, 7, 3, 5, 0, 4)
PLACE = tuple(AT.index(r) for r in range(NY))
OWN = PLACE[0]
CHUNK = 2 * TOK


def split2(value):
    high = value.astype(BF16)
    return high, (value - high.astype(F32)).astype(BF16)


def split3(value):
    high = value.astype(BF16)
    rest = value - high.astype(F32)
    mid = rest.astype(BF16)
    return high, mid, (rest - mid.astype(F32)).astype(BF16)


def matmul(left, right):
    return jnp.dot(left, right, preferred_element_type=F32)


def matmul_nt(left, right):
    return lax.dot_general(left, right, (((1,), (1,)), ((), ())), preferred_element_type=F32)


def fold_rows(value, combine):
    return combine(value.reshape(value.shape[0] // 8, 8, value.shape[1]), axis=0)


def kernel(
    order_hbm, q_hbm, k_hbm, v_hbm, g_hbm, o_out, dq_out, dk_out, dv_out,
    order, q_own, g_own, q_t, g_t, keys, vals, qs, gs, kp, vp, kt, vt, qf, gf,
    scores, gw, p_hi, p_lo, t_hi, t_lo, max8, sum8, dot8, stats, dots, scaled,
    dv_part, dk_part, o_part, dq_part, dv_in, dv_half, dk_in, dk_half, o_in, dq_in,
    local_sem, qx_s, qx_r, gx_s, gx_r, ky_s, ky_r, vy_s, vy_r, st_s, st_r, rd_s, rd_r,
    dvy_s, dvy_r, dky_s, dky_r, ox_s, ox_r, dqx_s, dqx_r,
):
    seqs = lax.axis_size("outer") // GROUPS
    outer = lax.axis_index("outer")
    inner = lax.axis_index("inner")
    seq = lax.rem(outer, seqs)
    x = lax.rem(inner, NX)
    y = (inner // NX) * GROUPS + outer // seqs

    def device(at_x, at_y):
        return (lax.rem(at_y, GROUPS) * seqs + seq, (at_y // GROUPS) * NX + at_x)

    def along_x(step):
        return device(lax.rem(x + step + NX, NX), y)

    def along_y(step):
        return device(x, lax.rem(y + step + NY, NY))

    def position(at_x, at_y):
        return order[lax.rem(at_y, GROUPS) * (NX * NY // GROUPS) + (at_y // GROUPS) * NX + at_x]

    def remote(src, dst, send, recv, where):
        return pltpu.make_async_remote_copy(
            src_ref=src, dst_ref=dst, send_sem=send, recv_sem=recv, device_id=where, device_id_type=MESH
        )

    up, down, up2, down2 = along_y(1), along_y(-1), along_y(2), along_y(-2)
    right, left, across = along_x(1), along_x(-1), along_x(2)
    peers = (right, across, left)

    loads = [
        pltpu.make_async_copy(q_hbm.at[0], q_own, local_sem.at[0]),
        pltpu.make_async_copy(g_hbm.at[0], g_own, local_sem.at[1]),
        pltpu.make_async_copy(k_hbm.at[0], keys.at[OWN], local_sem.at[2]),
        pltpu.make_async_copy(v_hbm.at[0], vals.at[OWN], local_sem.at[3]),
        pltpu.make_async_copy(order_hbm, order, local_sem.at[4]),
    ]
    for load in loads:
        load.start()
    barrier = pltpu.get_barrier_semaphore()
    for peer in (up, down, up2, down2, right, left, across):
        pl.semaphore_signal(barrier, inc=1, device_id=peer, device_id_type=MESH)
    pl.semaphore_wait(barrier, 7)

    ways = ((1, up, up2), (-1, down, down2))

    def gather_y(own, buf, send, recv, by_two):
        copies = {}
        for d, (sign, near, far) in enumerate(ways):
            at = [buf.at[PLACE[(sign * n) % NY]] for n in range(5)]
            rows = pl.ds(d * HALF, HALF)
            copies[d, 1] = remote(own, at[1], send.at[4 * d], recv.at[4 * d], near)
            if by_two:
                copies[d, 2] = remote(own, at[2], send.at[4 * d + 1], recv.at[4 * d + 1], far)
            else:
                copies[d, 2] = remote(at[1], at[2], send.at[4 * d + 1], recv.at[4 * d + 1], near)
            copies[d, 3] = remote(at[2], at[3], send.at[4 * d + 2], recv.at[4 * d + 2], near)
            copies[d, 4] = remote(at[2].at[rows], at[4].at[rows], send.at[4 * d + 3], recv.at[4 * d + 3], far)
        return copies

    def gather_x(buf, send, recv):
        return [
            remote(buf.at[0], buf.at[n + 1], send.at[n], recv.at[n], peers[n]) for n in range(NX - 1)
        ]

    k_go, v_go = gather_y(k_hbm.at[0], keys, ky_s, ky_r, True), gather_y(v_hbm.at[0], vals, vy_s, vy_r, False)
    q_go, g_go = gather_x(q_t, qx_s, qx_r), gather_x(g_t, gx_s, gx_r)
    gathered = [*k_go.values(), *v_go.values(), *q_go, *g_go]
    everything = []

    def start(copies, n):
        for d in range(2):
            copies[d, n].start()

    def arrived(copies, n):
        for d in range(2):
            copies[d, n].wait_recv()

    def ready_query(s):
        cols = pl.ds(s * QCOLS, QCOLS)
        q0, q1, q2 = split3(q_t[s])
        for n, piece in enumerate((q0, q1, q0, q1, q0, q2)):
            qs[n * HD:(n + 1) * HD, cols] = piece

    def ready_cotangent(s):
        cols = pl.ds(s * QCOLS, QCOLS)
        g0, g1 = split2(g_t[s])
        for n, piece in enumerate((g0, g1, g0)):
            gs[n * HD:(n + 1) * HD, cols] = piece

    def ready_key(place):
        rows = pl.ds(place * TOK, TOK)
        k0, k1, k2 = split3(keys[place])
        for n, piece in enumerate((k0, k0, k1, k1, k2, k0)):
            kp[rows, n * HD:(n + 1) * HD] = piece
        high, low = split2(keys[place].T)
        kt[0:HD, rows] = high
        kt[HD:2 * HD, rows] = low

    def ready_value(place):
        rows = pl.ds(place * TOK, TOK)
        v0, v1 = split2(vals[place])
        for n, piece in enumerate((v0, v0, v1)):
            vp[rows, n * HD:(n + 1) * HD] = piece
        high, low = split2(vals[place].T)
        vt[0:HD, rows] = high
        vt[HD:2 * HD, rows] = low

    def score_chunk(c):
        rows = pl.ds(c * CHUNK, CHUNK)
        for s in range(NX):
            cols = pl.ds(s * QCOLS, QCOLS)
            query_at = position(lax.rem(x - s + NX, NX), y)
            tile = matmul(kp[rows, :], qs[:, cols])
            parts = []
            for n in range(2):
                r = AT[2 * c + n]
                part = tile[n * TOK:(n + 1) * TOK]
                if r == 0 and s == 0:
                    key_at = lax.broadcasted_iota(jnp.int32, (TOK, QCOLS), 0)
                    token = lax.rem(lax.broadcasted_iota(jnp.int32, (TOK, QCOLS), 1), TOK)
                    part = jnp.where(key_at <= token, part, FAR)
                else:
                    seen = position(x, lax.rem(y - r + NY, NY)) <= query_at
                    part = part + jnp.where(seen, 0.0, FAR).astype(F32)
                parts.append(part)
            for n, part in enumerate(parts):
                scores[c * CHUNK + n * TOK:c * CHUNK + (n + 1) * TOK, cols] = part
            top = jnp.maximum(fold_rows(parts[0], jnp.max), fold_rows(parts[1], jnp.max))
            max8[:, cols] = top if c == 0 else jnp.maximum(max8[:, cols], top)

    start(k_go, 2)
    start(k_go, 1)
    loads[0].wait()
    for h in range(HEADS):
        q_t[0, :, h * TOK:(h + 1) * TOK] = q_own[:, h * HD:(h + 1) * HD].T * (SCALE * LOG2E)
    for n in (1, 0, 2):
        q_go[n].start()
    start(v_go, 1)
    loads[1].wait()
    for h in range(HEADS):
        g_t[0, :, h * TOK:(h + 1) * TOK] = g_own[:, h * HD:(h + 1) * HD].T
    for n in (1, 0, 2):
        g_go[n].start()
    for load in loads[2:]:
        load.wait()
    ready_query(0)
    ready_key(OWN)
    ready_cotangent(0)
    ready_value(OWN)

    arrived(k_go, 2)
    start(k_go, 4)
    start(k_go, 3)
    ready_key(0)
    ready_key(1)
    arrived(k_go, 1)
    ready_key(2)
    ready_key(3)
    q_go[0].wait_recv()
    ready_query(1)
    q_go[2].wait_recv()
    ready_query(3)
    arrived(v_go, 1)
    start(v_go, 2)
    q_go[1].wait_recv()
    ready_query(2)
    score_chunk(0)
    score_chunk(1)
    arrived(k_go, 3)
    ready_key(4)
    ready_key(5)
    score_chunk(2)
    arrived(k_go, 4)
    ready_key(7)
    score_chunk(3)
    arrived(v_go, 2)
    start(v_go, 4)
    start(v_go, 3)

    top = jnp.max(max8[...], axis=0, keepdims=True)
    def soft_chunk(c):
        rows = pl.ds(c * CHUNK, CHUNK)
        for s in range(NX):
            cols = pl.ds(s * QCOLS, QCOLS)
            weight = jnp.exp2(scores[rows, cols] - top[:, s * QCOLS:(s + 1) * QCOLS])
            scores[rows, cols] = weight
            high, low = split2(weight)
            p_hi[rows, cols] = high
            p_lo[rows, cols] = low
            part = fold_rows(weight, jnp.sum)
            sum8[:, cols] = part if c == 0 else sum8[:, cols] + part

    for c in range(NY // 2):
        soft_chunk(c)
    stats[0, 0:1, :] = top
    stats[0, 1:2, :] = jnp.sum(sum8[...], axis=0, keepdims=True)
    st_go = [
        remote(stats.at[0], stats.at[n + 1], st_s.at[n], st_r.at[n], peers[n]) for n in range(NX - 1)
    ]
    for copy in st_go:
        copy.start()

    for place in range(4):
        ready_value(place)
    for n in range(NX - 1):
        g_go[n].wait_recv()
        ready_cotangent(n + 1)

    def weigh_chunk(c):
        rows = pl.ds(c * CHUNK, CHUNK)
        for s in range(NX):
            cols = pl.ds(s * QCOLS, QCOLS)
            tile = matmul(vp[rows, :], gs[:, cols])
            gw[rows, cols] = tile
            part = fold_rows(tile * scores[rows, cols], jnp.sum)
            dot8[:, cols] = part if c == 0 else dot8[:, cols] + part

    weigh_chunk(0)
    weigh_chunk(1)

    def aligned(row, n):
        cut = ALLQ - (n + 1) * QCOLS
        return jnp.concatenate([row[:, cut:], row[:, :cut]], axis=1)

    for copy in st_go:
        copy.wait_recv()
    tops = [aligned(stats[n + 1, 0:1, :], n) for n in range(NX - 1)]
    whole_top = jnp.maximum(jnp.maximum(top, tops[0]), jnp.maximum(tops[1], tops[2]))
    own_factor = jnp.exp2(top - whole_top)
    total = own_factor * stats[0, 1:2, :]
    for n in range(NX - 1):
        total = total + jnp.exp2(tops[n] - whole_top) * aligned(stats[n + 1, 1:2, :], n)
    factor = own_factor / total
    scaled[...] = factor

    for s in range(NX):
        cols = pl.ds(s * QCOLS, QCOLS)
        row = scaled[:, cols]
        high, low = split2(g_t[s] * row)
        gf[0:HD, cols] = high
        gf[HD:2 * HD, cols] = low
        high, low = split2(q_t[s] * row)
        qf[0:HD, cols] = high
        qf[HD:2 * HD, cols] = low

    def key_side(c, high, low, right_side, part):
        rows = pl.ds(c * CHUNK, CHUNK)
        both = matmul_nt(high[rows, :], right_side[...]) + matmul_nt(low[rows, :], right_side[...])
        whole = both[:, :HD] + both[:, HD:]
        part[2 * c] = whole[:TOK]
        part[2 * c + 1] = whole[TOK:]

    def back_y(part, whole_in, half_in, send, recv, by_two):
        copies = {}
        for d, (sign, near, far) in enumerate(ways):
            at = [part.at[PLACE[(-sign * n) % NY]] for n in range(5)]
            rows = pl.ds(d * HALF, HALF)
            sems = [(send.at[4 * d + n], recv.at[4 * d + n]) for n in range(4)]
            copies[d, 4] = remote(at[4].at[rows], half_in.at[d], *sems[3], far)
            copies[d, 3] = remote(at[3], whole_in.at[d], *sems[2], near)
            copies[d, 2] = remote(at[2], whole_in.at[2 + d], *sems[1], far if by_two else near)
            copies[d, 1] = remote(at[1], whole_in.at[4 + d], *sems[0], near)
        return copies

    def join_far(copies, part, whole_in, half_in):
        for d, (sign, _, _) in enumerate(ways):
            place = PLACE[(-sign * 2) % NY]
            copies[d, 3].wait_recv()
            part[place] = part[place] + whole_in[d]
            copies[d, 4].wait_recv()
            rows = pl.ds(d * HALF, HALF)
            part[place, rows, :] = part[place, rows, :] + half_in[d]
            copies[d, 2].start()

    def join_near(copies, part, whole_in):
        for d, (sign, _, _) in enumerate(ways):
            place = PLACE[(-sign) % NY]
            copies[d, 2].wait_recv()
            part[place] = part[place] + whole_in[2 + d]
            copies[d, 1].start()

    def back_x(part, into, send, recv):
        return [
            remote(part.at[NX - 1 - n], into.at[n], send.at[n], recv.at[n], peers[n]) for n in range(NX - 1)
        ]

    dv_go = back_y(dv_part, dv_in, dv_half, dvy_s, dvy_r, False)
    dk_go = back_y(dk_part, dk_in, dk_half, dky_s, dky_r, True)
    o_go = back_x(o_part, o_in, ox_s, ox_r)
    dq_go = back_x(dq_part, dq_in, dqx_s, dqx_r)
    everything += [*dv_go.values(), *dk_go.values(), *o_go, *dq_go]

    key_side(2, p_hi, p_lo, gf, dv_part)
    start(dv_go, 3)
    key_side(3, p_hi, p_lo, gf, dv_part)
    start(dv_go, 4)
    key_side(0, p_hi, p_lo, gf, dv_part)

    arrived(v_go, 3)
    ready_value(4)
    ready_value(5)
    weigh_chunk(2)
    arrived(v_go, 4)
    ready_value(7)
    weigh_chunk(3)
    dots[0] = jnp.sum(dot8[...], axis=0, keepdims=True) * scaled[...]
    rd_go = [
        remote(dots.at[0], dots.at[n + 1], rd_s.at[n], rd_r.at[n], peers[n]) for n in range(NX - 1)
    ]
    everything += rd_go
    for copy in rd_go:
        copy.start()
    key_side(1, p_hi, p_lo, gf, dv_part)

    def query_side(s, sides, high, low, part, scale):
        cols = pl.ds(s * QCOLS, QCOLS)
        both = matmul(sides[...], high[:, cols]) + matmul(sides[...], low[:, cols])
        part[s] = (both[:HD] + both[HD:]) * (scaled[:, cols] * scale)

    for n in (1, 0, 2):
        query_side(NX - 1 - n, vt, p_hi, p_lo, o_part, 1.0)
        o_go[n].start()
    query_side(0, vt, p_hi, p_lo, o_part, 1.0)

    for copy in [*gathered, *st_go]:
        copy.wait_send()
    for copy in rd_go:
        copy.wait_recv()
    row_dot = dots[0]
    for n in range(NX - 1):
        row_dot = row_dot + aligned(dots[n + 1], n)

    def grad_chunk(c):
        rows = pl.ds(c * CHUNK, CHUNK)
        for s in range(NX):
            cols = pl.ds(s * QCOLS, QCOLS)
            value = scores[rows, cols] * (gw[rows, cols] - row_dot[:, s * QCOLS:(s + 1) * QCOLS])
            high, low = split2(value)
            t_hi[rows, cols] = high
            t_lo[rows, cols] = low

    grad_chunk(2)
    key_side(2, t_hi, t_lo, qf, dk_part)
    start(dk_go, 3)
    grad_chunk(3)
    key_side(3, t_hi, t_lo, qf, dk_part)
    start(dk_go, 4)
    join_far(dv_go, dv_part, dv_in, dv_half)
    grad_chunk(0)
    key_side(0, t_hi, t_lo, qf, dk_part)
    grad_chunk(1)
    for n in (1, 0, 2):
        query_side(NX - 1 - n, kt, t_hi, t_lo, dq_part, SCALE)
        dq_go[n].start()
    key_side(1, t_hi, t_lo, qf, dk_part)
    start(dk_go, 1)
    join_far(dk_go, dk_part, dk_in, dk_half)
    join_near(dv_go, dv_part, dv_in)
    query_side(0, kt, t_hi, t_lo, dq_part, SCALE)

    def finish_x(copies, part, full_in, out):
        for copy in copies:
            copy.wait_recv()
        whole = (part[0] + full_in[0]) + (full_in[1] + full_in[2])
        for h in range(HEADS):
            out[0, :, h * HD:(h + 1) * HD] = whole[:, h * TOK:(h + 1) * TOK].T

    finish_x(o_go, o_part, o_in, o_out)
    arrived(dv_go, 1)
    dv_out[0] = dv_part[OWN] + (dv_in[4] + dv_in[5])
    finish_x(dq_go, dq_part, dq_in, dq_out)
    arrived(dk_go, 2)
    arrived(dk_go, 1)
    dk_out[0] = (dk_part[OWN] + ((dk_in[2] + dk_in[3]) + (dk_in[4] + dk_in[5]))) * LN2
    for copy in everything:
        copy.wait_send()


def store(*refs):
    sources, targets, sems = refs[:4], refs[4:8], refs[8]
    copies = [pltpu.make_async_copy(a, b, sems.at[n]) for n, (a, b) in enumerate(zip(sources, targets))]
    for copy in copies:
        copy.start()
    for copy in copies:
        copy.wait()


def body(queries, key_rows, value_rows, cotangent, block_order):
    def vmem(*shape, dtype=F32):
        return pltpu.VMEM(shape, dtype)

    dma = lambda n: pltpu.SemaphoreType.DMA((n,))
    in_vmem = pl.BlockSpec(memory_space=pltpu.VMEM)
    in_hbm = pl.BlockSpec(memory_space=pltpu.HBM)
    wide = jax.ShapeDtypeStruct((1, TOK, HEADS * HD), F32)
    narrow = jax.ShapeDtypeStruct((1, TOK, HD), F32)
    shapes = (wide, wide, narrow, narrow)
    results = pl.pallas_call(
        kernel,
        out_shape=shapes,
        in_specs=[in_hbm] * 5,
        out_specs=[in_vmem] * 4,
        scratch_shapes=[
            pltpu.SMEM((NX * NY,), jnp.int32), vmem(TOK, HEADS * HD), vmem(TOK, HEADS * HD),
            vmem(NX, HD, QCOLS), vmem(NX, HD, QCOLS),
            vmem(NY, TOK, HD), vmem(NY, TOK, HD),
            vmem(6 * HD, ALLQ, dtype=BF16), vmem(3 * HD, ALLQ, dtype=BF16),
            vmem(ALLK, 6 * HD, dtype=BF16), vmem(ALLK, 3 * HD, dtype=BF16),
            vmem(2 * HD, ALLK, dtype=BF16), vmem(2 * HD, ALLK, dtype=BF16),
            vmem(2 * HD, ALLQ, dtype=BF16), vmem(2 * HD, ALLQ, dtype=BF16),
            vmem(ALLK, ALLQ), vmem(ALLK, ALLQ),
            vmem(ALLK, ALLQ, dtype=BF16), vmem(ALLK, ALLQ, dtype=BF16),
            vmem(ALLK, ALLQ, dtype=BF16), vmem(ALLK, ALLQ, dtype=BF16),
            vmem(8, ALLQ), vmem(8, ALLQ), vmem(8, ALLQ),
            vmem(NX, 2, ALLQ), vmem(NX, 1, ALLQ), vmem(1, ALLQ),
            vmem(NY, TOK, HD), vmem(NY, TOK, HD),
            vmem(NX, HD, QCOLS), vmem(NX, HD, QCOLS),
            vmem(6, TOK, HD), vmem(2, HALF, HD), vmem(6, TOK, HD), vmem(2, HALF, HD),
            vmem(3, HD, QCOLS), vmem(3, HD, QCOLS),
            dma(5),
            dma(3), dma(3), dma(3), dma(3), dma(8), dma(8), dma(8), dma(8),
            dma(3), dma(3), dma(3), dma(3),
            dma(8), dma(8), dma(8), dma(8), dma(3), dma(3), dma(3), dma(3),
        ],
        compiler_params=pltpu.CompilerParams(
            collective_id=0, has_side_effects=True, vmem_limit_bytes=44 * 1024 * 1024
        ),
    )(*(pltpu.with_memory_space_constraint(a, pltpu.HBM) for a in (block_order, queries, key_rows, value_rows, cotangent)))
    return pl.pallas_call(
        store,
        out_shape=shapes,
        in_specs=[in_vmem] * 4,
        out_specs=[in_hbm] * 4,
        scratch_shapes=[dma(4)],
    )(*results)


def solution(mesh):
    spread = P("outer", "inner", None)
    return jax.shard_map(
        body,
        mesh=mesh,
        in_specs=(spread, spread, spread, spread, P()),
        out_specs=(spread, spread, spread, spread),
        check_vma=False,
    )
```

time: 64.2 us -> 48.7 us (0.76)
  the two profiles are of different devices: /device:TPU:384 before, /device:TPU:8 now
where the time goes in v2:
time: 48.7 us; the launch traced here: 48.5 us
  Pallas kernels  45.3 us (93%)
  local copies, waits for them, and re-layouts  2.53 us (5%)
  between operations  0.65 us (1%)
    pallas_call x1, Pallas kernels, body(): pl.pallas_call(kernel, out_shape=shapes, in_specs=[in_hbm] * 5, out_specs...  43.6 us
    unnamed x8, local copies, waits for them, and re-layouts  2.53 us
    pallas_call x1, Pallas kernels, body(): pl.pallas_call(store, out_shape=shapes, in_specs=[in_vmem] * 4, out_specs...  1.77 us

profile of v2, /device:TPU:8, one launch (start us, length us, event | category | flops | bytes accessed | tf_op | source)
XLA Modules:
  0.0 48.5 jit_solution(16067497234844461675)
XLA Ops:
  0.6 43.6 %shard_map.84 = (f32[1,128,256]{2,1,0:T(8,128)S(1)}, f32[1,128,256]{2,1,0:T(8,128)S(1)}, f32[1,128,128]{2,1,0:T(8,128)S(1)}, f32[1,128,128]{2,1,0:T(8,128)S(1)}) custom-call(s32[32]{0:T(128)} %order_hbm.1, f32[1,128,256]{2,1,0:T(8,128)} %q_hbm.1, f32[1,128,128]{2,1,0:T(8,128)} %k_hbm.1, f32[1,128,128]{2,1,0:T(8,128)} %v_hbm.1, f32[1,128,256]{2,1,0:T(8,128)} %g_hbm.1), custom_call_target="tpu_custom_call" | custom-call | tf_op jit(solution)/shard_map/pallas_call | solution.py:460
  44.2 0.0 copy-start
  44.2 0.6 %copy-done = f32[1,128,256]{2,1,0:T(8,128)} copy-done((f32[1,128,256]{2,1,0:T(8,128)}, f32[1,128,256]{2,1,0:T(8,128)S(1)}, u32[]{:S(2)}) %copy-start) | copy-done | bytes 131096
  44.9 0.0 copy-start.1
  44.9 0.6 %copy-done.1 = f32[1,128,256]{2,1,0:T(8,128)} copy-done((f32[1,128,256]{2,1,0:T(8,128)}, f32[1,128,256]{2,1,0:T(8,128)S(1)}, u32[]{:S(2)}) %copy-start.1) | copy-done | bytes 131096
  45.5 0.0 copy-start.2
  45.5 0.6 %copy-done.2 = f32[1,128,128]{2,1,0:T(8,128)} copy-done((f32[1,128,128]{2,1,0:T(8,128)}, f32[1,128,128]{2,1,0:T(8,128)S(1)}, u32[]{:S(2)}) %copy-start.2) | copy-done | bytes 65560
  46.1 0.0 copy-start.3
  46.1 0.6 %copy-done.3 = f32[1,128,128]{2,1,0:T(8,128)} copy-done((f32[1,128,128]{2,1,0:T(8,128)}, f32[1,128,128]{2,1,0:T(8,128)S(1)}, u32[]{:S(2)}) %copy-start.3) | copy-done | bytes 65560
  46.8 1.8 %shard_map.85 = (f32[1,128,256]{2,1,0:T(8,128)}, f32[1,128,256]{2,1,0:T(8,128)}, f32[1,128,128]{2,1,0:T(8,128)}, f32[1,128,128]{2,1,0:T(8,128)}) custom-call(f32[1,128,256]{2,1,0:T(8,128)} %copy-done, f32[1,128,256]{2,1,0:T(8,128)} %copy-done.1, f32[1,128,128]{2,1,0:T(8,128)} %copy-done.2, f32[1,128,128]{2,1,0:T(8,128)} %copy-done.3), custom_call_target="tpu_custom_call" | custom-call | tf_op jit(solution)/shard_map/pallas_call | solution.py:491
Async XLA Ops:
  44.2 0.7 %copy-start = (f32[1,128,256]{2,1,0:T(8,128)}, f32[1,128,256]{2,1,0:T(8,128)S(1)}, u32[]{:S(2)}) copy-start(f32[1,128,256]{2,1,0:T(8,128)S(1)} %get-tuple-element.8.refs_0_) | copy-start | bytes 393220
  44.9 0.6 %copy-start.1 = (f32[1,128,256]{2,1,0:T(8,128)}, f32[1,128,256]{2,1,0:T(8,128)S(1)}, u32[]{:S(2)}) copy-start(f32[1,128,256]{2,1,0:T(8,128)S(1)} %get-tuple-element.9.refs_1_) | copy-start | bytes 393220
  45.5 0.6 %copy-start.2 = (f32[1,128,128]{2,1,0:T(8,128)}, f32[1,128,128]{2,1,0:T(8,128)S(1)}, u32[]{:S(2)}) copy-start(f32[1,128,128]{2,1,0:T(8,128)S(1)} %get-tuple-element.10.refs_2_) | copy-start | bytes 196612
  46.1 0.6 %copy-start.3 = (f32[1,128,128]{2,1,0:T(8,128)}, f32[1,128,128]{2,1,0:T(8,128)S(1)}, u32[]{:S(2)}) copy-start(f32[1,128,128]{2,1,0:T(8,128)S(1)} %get-tuple-element.11.refs_3_) | copy-start | bytes 196612

commit v3 on v2

--- a/solution.py
+++ b/solution.py
@@ -494,7 +494,7 @@
         in_specs=[in_vmem] * 4,
         out_specs=[in_hbm] * 4,
         scratch_shapes=[dma(4)],
-    )(*results)
+    )(*(pltpu.with_memory_space_constraint(a, pltpu.VMEM) for a in results))
 
 
 def solution(mesh):

time: 48.7 us -> 45.1 us (0.926)
  local copies, waits for them, and re-layouts: 2.53 us -> 0 us
  Pallas kernels: 45.3 us -> 44.4 us
    unnamed x8 -> x0, local copies, waits for them, and re-layouts: 2.53 us -> none
    pallas_call x1, Pallas kernels: 1.77 us -> 0.77 us  [body(): pl.pallas_call(store, out_shape=shapes, in_specs=[in_vmem] * 4, out_specs...]
where the time goes in v3:
time: 45.1 us; the launch traced here: 45 us
  Pallas kernels  44.4 us (98%)
  between operations  0.64 us (1%)
    pallas_call x1, Pallas kernels, body(): pl.pallas_call(kernel, out_shape=shapes, in_specs=[in_hbm] * 5, out_specs...  43.6 us

profile of v3, /device:TPU:8, one launch (start us, length us, event | category | flops | bytes accessed | tf_op | source)
XLA Modules:
  0.0 45.0 jit_solution(7380978597878978863)
XLA Ops:
  0.6 43.6 %shard_map.84 = (f32[1,128,256]{2,1,0:T(8,128)S(1)}, f32[1,128,256]{2,1,0:T(8,128)S(1)}, f32[1,128,128]{2,1,0:T(8,128)S(1)}, f32[1,128,128]{2,1,0:T(8,128)S(1)}) custom-call(s32[32]{0:T(128)} %order_hbm.1, f32[1,128,256]{2,1,0:T(8,128)} %q_hbm.1, f32[1,128,128]{2,1,0:T(8,128)} %k_hbm.1, f32[1,128,128]{2,1,0:T(8,128)} %v_hbm.1, f32[1,128,256]{2,1,0:T(8,128)} %g_hbm.1), custom_call_target="tpu_custom_call" | custom-call | tf_op jit(solution)/shard_map/pallas_call | solution.py:460
  44.2 0.8 %shard_map.85 = (f32[1,128,256]{2,1,0:T(8,128)}, f32[1,128,256]{2,1,0:T(8,128)}, f32[1,128,128]{2,1,0:T(8,128)}, f32[1,128,128]{2,1,0:T(8,128)}) custom-call(f32[1,128,256]{2,1,0:T(8,128)S(1)} %get-tuple-element.8.refs_0_, f32[1,128,256]{2,1,0:T(8,128)S(1)} %get-tuple-element.9.refs_1_, f32[1,128,128]{2,1,0:T(8,128)S(1)} %get-tuple-element.10.refs_2_, ...), custom_call_target="tpu_custom_call" | custom-call | tf_op jit(solution)/shard_map/pallas_call | solution.py:491

commit v4 on v3

--- a/solution.py
+++ b/solution.py
@@ -201,8 +201,6 @@
     loads[1].wait()
     for h in range(HEADS):
         g_t[0, :, h * TOK:(h + 1) * TOK] = g_own[:, h * HD:(h + 1) * HD].T
-    for n in (1, 0, 2):
-        g_go[n].start()
     for load in loads[2:]:
         load.wait()
     ready_query(0)
@@ -218,13 +216,15 @@
     arrived(k_go, 1)
     ready_key(2)
     ready_key(3)
+    arrived(v_go, 1)
+    start(v_go, 2)
     q_go[0].wait_recv()
     ready_query(1)
     q_go[2].wait_recv()
     ready_query(3)
-    arrived(v_go, 1)
-    start(v_go, 2)
     q_go[1].wait_recv()
+    for n in (1, 0, 2):
+        g_go[n].start()
     ready_query(2)
     score_chunk(0)
     score_chunk(1)
@@ -233,12 +233,11 @@
     ready_key(5)
     score_chunk(2)
     arrived(k_go, 4)
-    ready_key(7)
-    score_chunk(3)
     arrived(v_go, 2)
     start(v_go, 4)
     start(v_go, 3)
-
+    ready_key(7)
+    score_chunk(3)
     top = jnp.max(max8[...], axis=0, keepdims=True)
     def soft_chunk(c):
         rows = pl.ds(c * CHUNK, CHUNK)
@@ -301,9 +300,6 @@
         high, low = split2(g_t[s] * row)
         gf[0:HD, cols] = high
         gf[HD:2 * HD, cols] = low
-        high, low = split2(q_t[s] * row)
-        qf[0:HD, cols] = high
-        qf[HD:2 * HD, cols] = low
 
     def key_side(c, high, low, right_side, part):
         rows = pl.ds(c * CHUNK, CHUNK)
@@ -351,12 +347,6 @@
     o_go = back_x(o_part, o_in, ox_s, ox_r)
     dq_go = back_x(dq_part, dq_in, dqx_s, dqx_r)
     everything += [*dv_go.values(), *dk_go.values(), *o_go, *dq_go]
-
-    key_side(2, p_hi, p_lo, gf, dv_part)
-    start(dv_go, 3)
-    key_side(3, p_hi, p_lo, gf, dv_part)
-    start(dv_go, 4)
-    key_side(0, p_hi, p_lo, gf, dv_part)
 
     arrived(v_go, 3)
     ready_value(4)
@@ -372,7 +362,16 @@
     everything += rd_go
     for copy in rd_go:
         copy.start()
-    key_side(1, p_hi, p_lo, gf, dv_part)
+    key_side(2, p_hi, p_lo, gf, dv_part)
+    start(dv_go, 3)
+    key_side(3, p_hi, p_lo, gf, dv_part)
+    start(dv_go, 4)
+    key_side(0, p_hi, p_lo, gf, dv_part)
+    for s in range(NX):
+        cols = pl.ds(s * QCOLS, QCOLS)
+        high, low = split2(q_t[s] * scaled[:, cols])
+        qf[0:HD, cols] = high
+        qf[HD:2 * HD, cols] = low
 
     def query_side(s, sides, high, low, part, scale):
         cols = pl.ds(s * QCOLS, QCOLS)
@@ -382,10 +381,7 @@
     for n in (1, 0, 2):
         query_side(NX - 1 - n, vt, p_hi, p_lo, o_part, 1.0)
         o_go[n].start()
-    query_side(0, vt, p_hi, p_lo, o_part, 1.0)
-
-    for copy in [*gathered, *st_go]:
-        copy.wait_send()
+
     for copy in rd_go:
         copy.wait_recv()
     row_dot = dots[0]
@@ -408,6 +404,7 @@
     key_side(3, t_hi, t_lo, qf, dk_part)
     start(dk_go, 4)
     join_far(dv_go, dv_part, dv_in, dv_half)
+    key_side(1, p_hi, p_lo, gf, dv_part)
     grad_chunk(0)
     key_side(0, t_hi, t_lo, qf, dk_part)
     grad_chunk(1)
@@ -416,8 +413,11 @@
         dq_go[n].start()
     key_side(1, t_hi, t_lo, qf, dk_part)
     start(dk_go, 1)
+    for copy in [*gathered, *st_go]:
+        copy.wait_send()
     join_far(dk_go, dk_part, dk_in, dk_half)
     join_near(dv_go, dv_part, dv_in)
+    query_side(0, vt, p_hi, p_lo, o_part, 1.0)
     query_side(0, kt, t_hi, t_lo, dq_part, SCALE)
 
     def finish_x(copies, part, full_in, out):

time: 45.1 us -> 44 us (0.976)
  Pallas kernels: 44.4 us -> 43.2 us
    pallas_call x1, Pallas kernels: 43.6 us -> 42.5 us  [body(): pl.pallas_call(kernel, out_shape=shapes, in_specs=[in_hbm] * 5, out_specs...]
where the time goes in v4:
time: 44 us; the launch traced here: 43.9 us
  Pallas kernels  43.2 us (98%)
  between operations  0.64 us (1%)
    pallas_call x1, Pallas kernels, body(): pl.pallas_call(kernel, out_shape=shapes, in_specs=[in_hbm] * 5, out_specs...  42.5 us

profile of v4, /device:TPU:8, one launch (start us, length us, event | category | flops | bytes accessed | tf_op | source)
XLA Modules:
  0.0 43.9 jit_solution(15259275942294487648)
XLA Ops:
  0.6 42.5 %shard_map.84 = (f32[1,128,256]{2,1,0:T(8,128)S(1)}, f32[1,128,256]{2,1,0:T(8,128)S(1)}, f32[1,128,128]{2,1,0:T(8,128)S(1)}, f32[1,128,128]{2,1,0:T(8,128)S(1)}) custom-call(s32[32]{0:T(128)} %order_hbm.1, f32[1,128,256]{2,1,0:T(8,128)} %q_hbm.1, f32[1,128,128]{2,1,0:T(8,128)} %k_hbm.1, f32[1,128,128]{2,1,0:T(8,128)} %v_hbm.1, f32[1,128,256]{2,1,0:T(8,128)} %g_hbm.1), custom_call_target="tpu_custom_call" | custom-call | tf_op jit(solution)/shard_map/pallas_call | solution.py:460
  43.1 0.8 %shard_map.85 = (f32[1,128,256]{2,1,0:T(8,128)}, f32[1,128,256]{2,1,0:T(8,128)}, f32[1,128,128]{2,1,0:T(8,128)}, f32[1,128,128]{2,1,0:T(8,128)}) custom-call(f32[1,128,256]{2,1,0:T(8,128)S(1)} %get-tuple-element.8.refs_0_, f32[1,128,256]{2,1,0:T(8,128)S(1)} %get-tuple-element.9.refs_1_, f32[1,128,128]{2,1,0:T(8,128)S(1)} %get-tuple-element.10.refs_2_, ...), custom_call_target="tpu_custom_call" | custom-call | tf_op jit(solution)/shard_map/pallas_call | solution.py:491

commit v5 on v4

--- a/solution.py
+++ b/solution.py
@@ -127,7 +127,6 @@
     k_go, v_go = gather_y(k_hbm.at[0], keys, ky_s, ky_r, True), gather_y(v_hbm.at[0], vals, vy_s, vy_r, False)
     q_go, g_go = gather_x(q_t, qx_s, qx_r), gather_x(g_t, gx_s, gx_r)
     gathered = [*k_go.values(), *v_go.values(), *q_go, *g_go]
-    everything = []
 
     def start(copies, n):
         for d in range(2):
@@ -337,16 +336,41 @@
             part[place] = part[place] + whole_in[2 + d]
             copies[d, 1].start()
 
+    def back_halves(part, whole_in, half_in, send, recv):
+        copies = {}
+        for d, (sign, near, far) in enumerate(ways):
+            at = [part.at[PLACE[(-sign * n) % NY]] for n in range(5)]
+            sems = [(send.at[6 * d + n], recv.at[6 * d + n]) for n in range(6)]
+            copies[d, 1] = remote(at[1], whole_in.at[4 + d], *sems[0], near)
+            for n in range(2):
+                rows = pl.ds((1 - d if n == 0 else d) * HALF, HALF)
+                copies[d, 2, n] = remote(at[2].at[rows], whole_in.at[2 + d, rows], *sems[1 + n], far)
+                copies[d, 3, n] = remote(at[3].at[rows], whole_in.at[d, rows], *sems[3 + n], near)
+            copies[d, 4] = remote(at[4].at[rows], half_in.at[d], *sems[5], far)
+        return copies
+
+    def join_halves(copies, part, whole_in, half_in):
+        for n in range(2):
+            for d, (sign, _, _) in enumerate(ways):
+                place = PLACE[(-sign * 2) % NY]
+                rows = pl.ds((1 - d if n == 0 else d) * HALF, HALF)
+                copies[d, 3, n].wait_recv()
+                whole = part[place, rows, :] + whole_in[d, rows, :]
+                if n == 1:
+                    copies[d, 4].wait_recv()
+                    whole = whole + half_in[d]
+                part[place, rows, :] = whole
+                copies[d, 2, n].start()
+
     def back_x(part, into, send, recv):
         return [
             remote(part.at[NX - 1 - n], into.at[n], send.at[n], recv.at[n], peers[n]) for n in range(NX - 1)
         ]
 
     dv_go = back_y(dv_part, dv_in, dv_half, dvy_s, dvy_r, False)
-    dk_go = back_y(dk_part, dk_in, dk_half, dky_s, dky_r, True)
+    dk_go = back_halves(dk_part, dk_in, dk_half, dky_s, dky_r)
     o_go = back_x(o_part, o_in, ox_s, ox_r)
     dq_go = back_x(dq_part, dq_in, dqx_s, dqx_r)
-    everything += [*dv_go.values(), *dk_go.values(), *o_go, *dq_go]
 
     arrived(v_go, 3)
     ready_value(4)
@@ -359,13 +383,12 @@
     rd_go = [
         remote(dots.at[0], dots.at[n + 1], rd_s.at[n], rd_r.at[n], peers[n]) for n in range(NX - 1)
     ]
-    everything += rd_go
     for copy in rd_go:
         copy.start()
+    key_side(3, p_hi, p_lo, gf, dv_part)
+    start(dv_go, 4)
     key_side(2, p_hi, p_lo, gf, dv_part)
     start(dv_go, 3)
-    key_side(3, p_hi, p_lo, gf, dv_part)
-    start(dv_go, 4)
     key_side(0, p_hi, p_lo, gf, dv_part)
     for s in range(NX):
         cols = pl.ds(s * QCOLS, QCOLS)
@@ -397,25 +420,27 @@
             t_hi[rows, cols] = high
             t_lo[rows, cols] = low
 
-    grad_chunk(2)
-    key_side(2, t_hi, t_lo, qf, dk_part)
-    start(dk_go, 3)
     grad_chunk(3)
     key_side(3, t_hi, t_lo, qf, dk_part)
     start(dk_go, 4)
+    grad_chunk(2)
+    key_side(2, t_hi, t_lo, qf, dk_part)
+    for n in range(2):
+        for d in range(2):
+            dk_go[d, 3, n].start()
     join_far(dv_go, dv_part, dv_in, dv_half)
-    key_side(1, p_hi, p_lo, gf, dv_part)
+    grad_chunk(1)
+    key_side(1, t_hi, t_lo, qf, dk_part)
+    start(dk_go, 1)
     grad_chunk(0)
     key_side(0, t_hi, t_lo, qf, dk_part)
-    grad_chunk(1)
     for n in (1, 0, 2):
         query_side(NX - 1 - n, kt, t_hi, t_lo, dq_part, SCALE)
         dq_go[n].start()
-    key_side(1, t_hi, t_lo, qf, dk_part)
-    start(dk_go, 1)
+    key_side(1, p_hi, p_lo, gf, dv_part)
     for copy in [*gathered, *st_go]:
         copy.wait_send()
-    join_far(dk_go, dk_part, dk_in, dk_half)
+    join_halves(dk_go, dk_part, dk_in, dk_half)
     join_near(dv_go, dv_part, dv_in)
     query_side(0, vt, p_hi, p_lo, o_part, 1.0)
     query_side(0, kt, t_hi, t_lo, dq_part, SCALE)
@@ -430,11 +455,15 @@
     finish_x(o_go, o_part, o_in, o_out)
     arrived(dv_go, 1)
     dv_out[0] = dv_part[OWN] + (dv_in[4] + dv_in[5])
+    for copy in [*rd_go, *dv_go.values(), *o_go]:
+        copy.wait_send()
     finish_x(dq_go, dq_part, dq_in, dq_out)
-    arrived(dk_go, 2)
+    for n in range(2):
+        for d in range(2):
+            dk_go[d, 2, n].wait_recv()
     arrived(dk_go, 1)
     dk_out[0] = (dk_part[OWN] + ((dk_in[2] + dk_in[3]) + (dk_in[4] + dk_in[5]))) * LN2
-    for copy in everything:
+    for copy in [*dq_go, *dk_go.values()]:
         copy.wait_send()
 
 
@@ -482,7 +511,7 @@
             dma(5),
             dma(3), dma(3), dma(3), dma(3), dma(8), dma(8), dma(8), dma(8),
             dma(3), dma(3), dma(3), dma(3),
-            dma(8), dma(8), dma(8), dma(8), dma(3), dma(3), dma(3), dma(3),
+            dma(8), dma(8), dma(12), dma(12), dma(3), dma(3), dma(3), dma(3),
         ],
         compiler_params=pltpu.CompilerParams(
             collective_id=0, has_side_effects=True, vmem_limit_bytes=44 * 1024 * 1024

time: 44 us -> 42.9 us (0.975)
  Pallas kernels: 43.2 us -> 42.2 us
    pallas_call x1, Pallas kernels: 42.5 us -> 41.4 us  [body(): pl.pallas_call(kernel, out_shape=shapes, in_specs=[in_hbm] * 5, out_specs...]
where the time goes in v5:
time: 42.9 us; the launch traced here: 42.8 us
  Pallas kernels  42.2 us (98%)
  between operations  0.64 us (1%)
    pallas_call x1, Pallas kernels, body(): pl.pallas_call(kernel, out_shape=shapes, in_specs=[in_hbm] * 5, out_specs...  41.4 us

profile of v5, /device:TPU:8, one launch (start us, length us, event | category | flops | bytes accessed | tf_op | source)
XLA Modules:
  0.0 42.8 jit_solution(17995570606624894565)
XLA Ops:
  0.6 41.4 %shard_map.84 = (f32[1,128,256]{2,1,0:T(8,128)S(1)}, f32[1,128,256]{2,1,0:T(8,128)S(1)}, f32[1,128,128]{2,1,0:T(8,128)S(1)}, f32[1,128,128]{2,1,0:T(8,128)S(1)}) custom-call(s32[32]{0:T(128)} %order_hbm.1, f32[1,128,256]{2,1,0:T(8,128)} %q_hbm.1, f32[1,128,128]{2,1,0:T(8,128)} %k_hbm.1, f32[1,128,128]{2,1,0:T(8,128)} %v_hbm.1, f32[1,128,256]{2,1,0:T(8,128)} %g_hbm.1), custom_call_target="tpu_custom_call" | custom-call | tf_op jit(solution)/shard_map/pallas_call | solution.py:489
  42.0 0.8 %shard_map.85 = (f32[1,128,256]{2,1,0:T(8,128)}, f32[1,128,256]{2,1,0:T(8,128)}, f32[1,128,128]{2,1,0:T(8,128)}, f32[1,128,128]{2,1,0:T(8,128)}) custom-call(f32[1,128,256]{2,1,0:T(8,128)S(1)} %get-tuple-element.8.refs_0_, f32[1,128,256]{2,1,0:T(8,128)S(1)} %get-tuple-element.9.refs_1_, f32[1,128,128]{2,1,0:T(8,128)S(1)} %get-tuple-element.10.refs_2_, ...), custom_call_target="tpu_custom_call" | custom-call | tf_op jit(solution)/shard_map/pallas_call | solution.py:520

commit v6 on v5

--- a/solution.py
+++ b/solution.py
@@ -119,12 +119,26 @@
             copies[d, 4] = remote(at[2].at[rows], at[4].at[rows], send.at[4 * d + 3], recv.at[4 * d + 3], far)
         return copies
 
+    def gather_halves(own, buf, send, recv):
+        copies = {}
+        for d, (sign, near, far) in enumerate(ways):
+            at = [buf.at[PLACE[(sign * n) % NY]] for n in range(5)]
+            sems = [(send.at[6 * d + n], recv.at[6 * d + n]) for n in range(6)]
+            for n in range(2):
+                rows = pl.ds((d if n == 0 else 1 - d) * HALF, HALF)
+                copies[d, 1, n] = remote(own.at[rows], at[1].at[rows], *sems[n], near)
+                copies[d, 2, n] = remote(at[1].at[rows], at[2].at[rows], *sems[2 + n], near)
+            rows = pl.ds(d * HALF, HALF)
+            copies[d, 3] = remote(at[2], at[3], *sems[4], near)
+            copies[d, 4] = remote(at[2].at[rows], at[4].at[rows], *sems[5], far)
+        return copies
+
     def gather_x(buf, send, recv):
         return [
             remote(buf.at[0], buf.at[n + 1], send.at[n], recv.at[n], peers[n]) for n in range(NX - 1)
         ]
 
-    k_go, v_go = gather_y(k_hbm.at[0], keys, ky_s, ky_r, True), gather_y(v_hbm.at[0], vals, vy_s, vy_r, False)
+    k_go, v_go = gather_y(k_hbm.at[0], keys, ky_s, ky_r, True), gather_halves(v_hbm.at[0], vals, vy_s, vy_r)
     q_go, g_go = gather_x(q_t, qx_s, qx_r), gather_x(g_t, gx_s, gx_r)
     gathered = [*k_go.values(), *v_go.values(), *q_go, *g_go]
 
@@ -196,7 +210,9 @@
         q_t[0, :, h * TOK:(h + 1) * TOK] = q_own[:, h * HD:(h + 1) * HD].T * (SCALE * LOG2E)
     for n in (1, 0, 2):
         q_go[n].start()
-    start(v_go, 1)
+    for n in range(2):
+        for d in range(2):
+            v_go[d, 1, n].start()
     loads[1].wait()
     for h in range(HEADS):
         g_t[0, :, h * TOK:(h + 1) * TOK] = g_own[:, h * HD:(h + 1) * HD].T
@@ -215,8 +231,10 @@
     arrived(k_go, 1)
     ready_key(2)
     ready_key(3)
-    arrived(v_go, 1)
-    start(v_go, 2)
+    for n in range(2):
+        for d in range(2):
+            v_go[d, 1, n].wait_recv()
+            v_go[d, 2, n].start()
     q_go[0].wait_recv()
     ready_query(1)
     q_go[2].wait_recv()
@@ -232,9 +250,10 @@
     ready_key(5)
     score_chunk(2)
     arrived(k_go, 4)
-    arrived(v_go, 2)
-    start(v_go, 4)
-    start(v_go, 3)
+    for n, last in enumerate((4, 3)):
+        for d in range(2):
+            v_go[d, 2, n].wait_recv()
+            v_go[d, last].start()
     ready_key(7)
     score_chunk(3)
     top = jnp.max(max8[...], axis=0, keepdims=True)
@@ -509,7 +528,7 @@
             vmem(6, TOK, HD), vmem(2, HALF, HD), vmem(6, TOK, HD), vmem(2, HALF, HD),
             vmem(3, HD, QCOLS), vmem(3, HD, QCOLS),
             dma(5),
-            dma(3), dma(3), dma(3), dma(3), dma(8), dma(8), dma(8), dma(8),
+            dma(3), dma(3), dma(3), dma(3), dma(8), dma(8), dma(12), dma(12),
             dma(3), dma(3), dma(3), dma(3),
             dma(8), dma(8), dma(12), dma(12), dma(3), dma(3), dma(3), dma(3),
         ],

time: 42.9 us -> 42.6 us (level)
  the two profiles are of different devices: /device:TPU:8 before, /device:TPU:16 now
where the time goes in v6:
time: 42.6 us; the launch traced here: 42.5 us
  Pallas kernels  41.8 us (98%)
  between operations  0.64 us (2%)
    pallas_call x1, Pallas kernels, body(): pl.pallas_call(kernel, out_shape=shapes, in_specs=[in_hbm] * 5, out_specs...  41.1 us

profile of v6, /device:TPU:16, one launch (start us, length us, event | category | flops | bytes accessed | tf_op | source)
XLA Modules:
  0.0 42.5 jit_solution(17208495206007063415)
XLA Ops:
  0.6 41.1 %shard_map.84 = (f32[1,128,256]{2,1,0:T(8,128)S(1)}, f32[1,128,256]{2,1,0:T(8,128)S(1)}, f32[1,128,128]{2,1,0:T(8,128)S(1)}, f32[1,128,128]{2,1,0:T(8,128)S(1)}) custom-call(s32[32]{0:T(128)} %order_hbm.1, f32[1,128,256]{2,1,0:T(8,128)} %q_hbm.1, f32[1,128,128]{2,1,0:T(8,128)} %k_hbm.1, f32[1,128,128]{2,1,0:T(8,128)} %v_hbm.1, f32[1,128,256]{2,1,0:T(8,128)} %g_hbm.1), custom_call_target="tpu_custom_call" | custom-call | tf_op jit(solution)/shard_map/pallas_call | solution.py:508
  41.7 0.8 %shard_map.85 = (f32[1,128,256]{2,1,0:T(8,128)}, f32[1,128,256]{2,1,0:T(8,128)}, f32[1,128,128]{2,1,0:T(8,128)}, f32[1,128,128]{2,1,0:T(8,128)}) custom-call(f32[1,128,256]{2,1,0:T(8,128)S(1)} %get-tuple-element.8.refs_0_, f32[1,128,256]{2,1,0:T(8,128)S(1)} %get-tuple-element.9.refs_1_, f32[1,128,128]{2,1,0:T(8,128)S(1)} %get-tuple-element.10.refs_2_, ...), custom_call_target="tpu_custom_call" | custom-call | tf_op jit(solution)/shard_map/pallas_call | solution.py:539
